TPU v7x, 32 devices: a whole 2x2x4 slice. The times are simulated.
32 devices in a mesh: frag: 2 (over x), tile: 16 (over z, y, core).
Axes of the slice: x: 2, y: 2, z: 4, core: 2. Of those that a mesh axis runs over, the one named last changes fastest.
Arguments:
- amps: bfloat16 [32, 16, 16, 1024], P(('frag', 'tile')), parts along dimension 0, may hold values from -6 to 6
- ladder_ints: bfloat16 [32, 1024, 1024], P(('frag', 'tile')), parts along dimension 0, may hold values from -0.1875 to 0.1875
- quad_pairs: int32 [32, 2], P(('frag', 'tile')), parts along dimension 0, may hold values from 0 to 15, as said below
- cycle_ints: bfloat16 [4096, 2048], P(('frag', 'tile')), parts along dimension 0, may hold values from -0.125 to 0.125
Outputs:
- residual: bfloat16 [32, 16, 16, 1024], P('frag', 'tile'), parts along dimension 0
There are 2 independent parts, one for each index of `frag`. A program takes and returns all parts, laid end to end along the dimension named above; each array names one. Nothing has to cross between parts.
Inputs may be any that keep to these rules, and one draw needn't show every extreme that they name: `quad_pairs`: each row names an output tile pair and an input tile pair; no two rows are equal; every tile pair is named as output by some row and as input by some row; each device holds 1 row and the matching integral tiles.
All inputs are finite; a program needn't handle non-finite values.
Results may differ from a plain program's by a relative error of at most 0.0053.
Values may be sent and summed in bfloat16 or wider, within the bound.
No kernel may reach another device: no remote copies, remote signals or barrier semaphores. Data moves between devices by JAX's collectives and lax.ppermute only.
A program may use at most 128 MiB of HBM per device.

v0:
```python
import jax
import jax.numpy as jnp
from jax import lax
from jax.sharding import PartitionSpec as P

TS = 32
VT = 4


def per_device(amps, ladder_ints, quad_pairs, cycle_ints):
    local_occ, all_occ, pair_tiles, tile_area = amps.shape
    members = lax.axis_size("tile")
    quad_slots = ladder_ints.shape[0]
    all_quads = lax.all_gather(quad_pairs, "tile", axis=0, tiled=True)
    wanted = jnp.take(amps, all_quads[:, 1], axis=2)
    wanted = wanted.reshape(local_occ, all_occ, members, quad_slots, tile_area)
    arrived = lax.all_to_all(wanted, "tile", split_axis=2, concat_axis=0, tiled=True)
    arrived = arrived.reshape(all_occ * all_occ, quad_slots, tile_area)
    partial_value = jnp.einsum(
        "pqx,qxy->qpy", arrived, ladder_ints, preferred_element_type=jnp.float32
    )
    partial_value = partial_value.astype(jnp.bfloat16).reshape(
        quad_slots, all_occ, members, local_occ, tile_area
    )
    amp_send = amps.reshape(local_occ, members, local_occ, pair_tiles * tile_area)
    amp_moved = lax.all_to_all(amp_send, "tile", split_axis=1, concat_axis=0, tiled=True)
    part_moved = lax.all_to_all(partial_value, "tile", split_axis=2, concat_axis=0, tiled=True)
    amp_cycle = amp_moved.reshape(all_occ, local_occ, pair_tiles, tile_area)
    part_moved = part_moved.reshape(all_quads.shape[0], all_occ, local_occ, tile_area)
    selector = (
        all_quads[:, 0][:, None] == jnp.arange(pair_tiles, dtype=jnp.int32)[None, :]
    ).astype(jnp.bfloat16)
    ladder = jnp.einsum("gr,gijx->ijrx", selector, part_moved, preferred_element_type=jnp.float32)
    updated = (amp_cycle.astype(jnp.float32) + ladder).astype(jnp.bfloat16)
    cycle_input = updated.reshape(all_occ, local_occ, VT, VT, TS, TS).transpose(0, 2, 4, 1, 3, 5)
    cycle_input = cycle_input.reshape(all_occ * VT * TS, local_occ * VT * TS)
    cycle = jnp.dot(
        lax.all_gather(cycle_ints, "tile", axis=0, tiled=True),
        cycle_input,
        preferred_element_type=jnp.float32,
    )
    cycle = cycle.reshape(all_occ, VT, TS, local_occ, VT, TS).transpose(0, 3, 1, 4, 2, 5)
    cycle = cycle.reshape(all_occ, local_occ, pair_tiles, tile_area)
    return (ladder + cycle).astype(jnp.bfloat16)


def solution(mesh):
    return jax.shard_map(
        per_device,
        mesh=mesh,
        in_specs=(
            P(("frag", "tile"), None, None, None),
            P(("frag", "tile"), None, None),
            P(("frag", "tile"), None),
            P(("frag", "tile"), None),
        ),
        out_specs=P("frag", "tile", None, None),
        check_vma=False,
    )
```

profile of v0, /device:TPU:0, one launch (start us, length us, event | category | flops | bytes accessed | tf_op | source)
XLA Modules:
  0.0 155.6 jit_solution(9017295705784253806)
XLA Ops:
  6.5 0.0 copy-start
  6.5 0.0 all-gather.3.cloned.1.call-start
  6.5 0.7 all-gather.3.cloned.1.call-update
  7.3 23.3 %all-gather = s32[16,1,2]{2,1,0:T(1,128)S(1)} all-gather(s32[1,1,2]{2,1,0:T(1,128)} %bitcast.91), channel_id=1, replica_groups=mesh['frag'=2,'tile'=16] {'tile'}, dimensions={0}, use_global_device_ids=true | all-gather | bytes 136 | tf_op jit(solution)/shard_map/all_gather | solution.py:14
  30.5 0.1 copy.21
  30.6 1.3 copy.40
  32.0 0.6 gather_fusion
  32.6 0.9 fusion.8
  33.5 4.2 %all-to-all-start = ((bf16[1,16,16,1,1024]{4,1,3,0,2:T(8,128)(2,1)}), bf16[1,16,16,1,1024]{4,1,3,0,2:T(8,128)(2,1)}, u32[]{:S(2)}, u32[]{:S(2)}) async-start(bf16[1,16,16,1,1024]{4,1,3,0,2:T(8,128)(2,1)} %fusion.8), calls=%async_computation | async-start | bytes 1048576 | tf_op jit(solution)/shard_map/all_to_all | solution.py:17
  37.8 2.1 %reshape.97 = bf16[1,16,1,16384]{3,2,0,1:T(2,128)(2,1)S(1)} reshape(bf16[1,16,16,1024]{3,2,1,0:T(8,128)(2,1)} %param.4) | data formatting | bytes 1048576 | tf_op jit(solution)/shard_map/reshape | solution.py:25
  39.9 0.6 broadcast.39
  40.5 4.6 %reduce.2 = bf16[16,16384]{1,0:T(8,128)(2,1)} reduce(bf16[16,1,1,16384]{3,2,1,0:T(2,128)(2,1)S(1)} %bitcast.85, bf16[]{:T(256)} %broadcast.39), dimensions={1,2}, to_apply=%bitcast.71.reduce_sub_computation | reduce | bytes 1048578
  45.2 2.4 %reshape.99 = bf16[16,2,8192]{2,1,0:T(2,128)(2,1)} reshape(bf16[16,16384]{1,0:T(8,128)(2,1)} %reduce.2) | data formatting | bytes 1048576
  47.5 6.3 %all-to-all-done = bf16[1,16,16,1,1024]{4,1,3,0,2:T(8,128)(2,1)} async-done(((bf16[1,16,16,1,1024]{4,1,3,0,2:T(8,128)(2,1)}), bf16[1,16,16,1,1024]{4,1,3,0,2:T(8,128)(2,1)}, u32[]{:S(2)}, u32[]{:S(2)}) %all-to-all-start) | async-done | bytes 524320 | tf_op jit(solution)/shard_map/all_to_all | solution.py:17
  53.8 12.7 %all-to-all-start.2 = ((bf16[16,2,8192]{2,1,0:T(2,128)(2,1)}), bf16[16,2,8192]{2,1,0:T(2,128)(2,1)S(1)}, u32[]{:S(2)}, u32[]{:S(2)}) async-start(bf16[16,2,8192]{2,1,0:T(2,128)(2,1)} %reshape.99), calls=%async_computation.2 | async-start | bytes 1048576 | tf_op jit(solution)/shard_map/all_to_all | solution.py:26
  66.6 0.0 copy-done
  66.6 1.7 %fusion.2 = bf16[256,1024]{1,0:T(8,128)(2,1)S(1)} fusion(bf16[256,1024]{1,0:T(8,128)(2,1)} %bitcast.10, bf16[1,1024,1024]{2,1,0:T(8,128)(2,1)S(1)} %copy-done), kind=kOutput, calls=%fused_computation.6 | convolution fusion | flops 537133056 | bytes 3145728 | tf_op jit(solution)/shard_map/pqx,qxy->qpy/dot_general | solution.py:19
  68.4 1.1 copy.24
  69.5 18.8 %all-to-all-done.2 = bf16[16,2,8192]{2,1,0:T(2,128)(2,1)S(1)} async-done(((bf16[16,2,8192]{2,1,0:T(2,128)(2,1)}), bf16[16,2,8192]{2,1,0:T(2,128)(2,1)S(1)}, u32[]{:S(2)}, u32[]{:S(2)}) %all-to-all-start.2) | async-done | bytes 524320 | tf_op jit(solution)/shard_map/all_to_all | solution.py:26
  88.3 0.0 copy-start.1
  88.3 0.8 copy-done.1
  89.1 9.6 %all-to-all-start.1 = ((bf16[1,16,16,1,1024]{4,1,3,0,2:T(8,128)(2,1)}), bf16[1,16,16,1,1024]{4,1,3,0,2:T(8,128)(2,1)}, u32[]{:S(2)}, u32[]{:S(2)}) async-start(bf16[1,16,16,1,1024]{4,1,3,0,2:T(8,128)(2,1)} %copy.24), calls=%async_computation.1 | async-start | bytes 1048576 | tf_op jit(solution)/shard_map/all_to_all | solution.py:27
  98.6 2.2 %reshape.100 = bf16[16,1,1,16384]{3,2,1,0:T(2,128)(2,1)S(1)} reshape(bf16[16,2,8192]{2,1,0:T(2,128)(2,1)} %copy-done.1) | data formatting | bytes 1048576
  100.9 3.1 %convert_reduce_fusion = f32[16,16384]{1,0:T(8,128)S(1)} fusion(bf16[16,1,1,16384]{3,2,1,0:T(2,128)(2,1)S(1)} %reshape.100), kind=kLoop, calls=%fused_computation.9 | loop fusion | flops 262144 | bytes 1572864 | tf_op jit(solution)/shard_map/convert_element_type | solution.py:34
  103.9 0.6 copy.30
  104.6 8.6 %all-to-all-done.1 = bf16[1,16,16,1,1024]{4,1,3,0,2:T(8,128)(2,1)} async-done(((bf16[1,16,16,1,1024]{4,1,3,0,2:T(8,128)(2,1)}), bf16[1,16,16,1,1024]{4,1,3,0,2:T(8,128)(2,1)}, u32[]{:S(2)}, u32[]{:S(2)}) %all-to-all-start.1) | async-done | bytes 524320 | tf_op jit(solution)/shard_map/all_to_all | solution.py:27
  113.1 2.6 %fusion.5 = (bf16[16,1,16,1024]{3,2,0,1:T(8,128)(2,1)}, f32[16,1,16,1024]{3,2,0,1:T(8,128)}) fusion(f32[2,8,16,1024]{3,2,1,0:T(8,128)S(1)} %copy.30, s32[16]{0:T(128)S(1)} %get-tuple-element.5, bf16[1,16,16,1,1024]{4,1,3,0,2:T(8,128)(2,1)} %all-to-all-done.1), kind=kOutput, calls=%fused_computation.8 | convolution fusion | flops 8913152 | bytes 3145792 | tf_op jit(solution)/shard_map/gr,gijx->ijrx/dot_general | solution.py:33
  115.8 3.7 %reshape.78 = bf16[16,1,4,4,32,32]{5,4,3,2,0,1:T(8,128)(2,1)} reshape(bf16[16,1,16,1024]{3,2,0,1:T(8,128)(2,1)} %get-tuple-element.7) | data formatting | bytes 1048576 | tf_op jit(solution)/shard_map/reshape | solution.py:35
  119.5 4.0 %copy.39 = bf16[16,1,4,4,32,32]{5,3,4,2,0,1:T(4,128)(2,1)} copy(bf16[16,1,4,4,32,32]{5,4,3,2,0,1:T(8,128)(2,1)} %reshape.78) | data formatting | bytes 1048576 | tf_op jit(solution)/shard_map/reshape | solution.py:35
  123.5 3.8 %reshape.79 = bf16[2048,128]{1,0:T(8,128)(2,1)} reshape(bf16[16,4,32,1,4,32]{5,4,2,1,0,3:T(4,128)(2,1)} %bitcast.84) | data formatting | bytes 1048576 | tf_op jit(solution)/shard_map/reshape | solution.py:36
  127.2 0.0 all-gather.3.cloned.1.call-done
  127.3 6.5 %convolution_bitcast_fusion = f32[2048,128]{0,1:T(8,128)S(1)} fusion(bf16[2048,128]{1,0:T(8,128)(2,1)} %reshape.79, bf16[2048,2048]{1,0:T(8,128)(2,1)} %all-gather.3.cloned.1.call-done), kind=kOutput, calls=%fused_computation.1 | convolution fusion | flops 1073741824 | bytes 9961472 | tf_op jit(solution)/shard_map/dot_general | solution.py:37
  133.7 3.5 %reshape.80 = f32[16,4,32,1,4,32]{2,1,0,5,4,3:T(4,128)} reshape(f32[2048,128]{0,1:T(8,128)S(1)} %convolution_bitcast_fusion) | data formatting | bytes 2097152 | tf_op jit(solution)/shard_map/reshape | solution.py:42
  137.3 5.6 %copy.28 = f32[16,4,32,1,4,32]{5,2,4,1,0,3:T(8,128)} copy(f32[16,4,32,1,4,32]{2,1,0,5,4,3:T(4,128)} %reshape.80) | data formatting | bytes 2097152 | tf_op jit(solution)/shard_map/reshape | solution.py:42
  142.9 3.7 %reshape.81 = f32[16,1,16,1024]{3,2,0,1:T(8,128)S(1)} reshape(f32[16,1,4,4,32,32]{5,4,3,2,0,1:T(8,128)} %bitcast.83) | data formatting | bytes 2097152 | tf_op jit(solution)/shard_map/reshape | solution.py:43
  146.6 2.1 %fusion.6 = bf16[16,1,16,1024]{3,2,1,0:T(8,128)(2,1)} fusion(f32[16,1,16,1024]{3,2,0,1:T(8,128)} %get-tuple-element.8, f32[16,1,16,1024]{3,2,0,1:T(8,128)S(1)} %reshape.81), kind=kLoop, calls=%fused_computation.11 | loop fusion | flops 524288 | bytes 2621440 | tf_op jit(solution)/shard_map/convert_element_type | solution.py:44
  (3 shorter events, 0.0 us)
Async XLA Ops:
  6.5 60.1 %copy-start = (bf16[1,1024,1024]{2,1,0:T(8,128)(2,1)S(1)}, bf16[1,1024,1024]{2,1,0:T(8,128)(2,1)}, u32[]{:S(2)}) copy-start(bf16[1,1024,1024]{2,1,0:T(8,128)(2,1)} %param.5) | copy-start | bytes 6291460
  6.5 120.7 %all-gather.3.cloned.1.call-start = ((), (), s32[]{:S(2)}) async-start(), calls=%async_computation.3 | async-start | bytes 8912896 | tf_op jit(solution)/shard_map/all_gather | solution.py:38
  33.5 20.3 %all-to-all-start = ((bf16[1,16,16,1,1024]{4,1,3,0,2:T(8,128)(2,1)}), bf16[1,16,16,1,1024]{4,1,3,0,2:T(8,128)(2,1)}, u32[]{:S(2)}, u32[]{:S(2)}) async-start(bf16[1,16,16,1,1024]{4,1,3,0,2:T(8,128)(2,1)} %fusion.8), calls=%async_computation | async-start | bytes 1048576 | tf_op jit(solution)/shard_map/all_to_all | solution.py:17
  53.8 34.4 %all-to-all-start.2 = ((bf16[16,2,8192]{2,1,0:T(2,128)(2,1)}), bf16[16,2,8192]{2,1,0:T(2,128)(2,1)S(1)}, u32[]{:S(2)}, u32[]{:S(2)}) async-start(bf16[16,2,8192]{2,1,0:T(2,128)(2,1)} %reshape.99), calls=%async_computation.2 | async-start | bytes 1048576 | tf_op jit(solution)/shard_map/all_to_all | solution.py:26
  88.3 0.8 copy-start.1
  89.1 24.1 %all-to-all-start.1 = ((bf16[1,16,16,1,1024]{4,1,3,0,2:T(8,128)(2,1)}), bf16[1,16,16,1,1024]{4,1,3,0,2:T(8,128)(2,1)}, u32[]{:S(2)}, u32[]{:S(2)}) async-start(bf16[1,16,16,1,1024]{4,1,3,0,2:T(8,128)(2,1)} %copy.24), calls=%async_computation.1 | async-start | bytes 1048576 | tf_op jit(solution)/shard_map/all_to_all | solution.py:27
Sparse Core Ops, SparseCore 0:
  9.5 90.4 all-gather.2
where the time goes:
time: 157 us; the launch traced here: 156 us
  local copies, waits for them, and re-layouts  36.2 us (23%)
  waiting for transfers between devices  34.4 us (22%)
  starting transfers between devices  26.5 us (17%)
  blocking collectives  23.3 us (15%)
  between operations  13.5 us (9%)
  matrix products  10.9 us (7%)
  other arithmetic  10.8 us (7%)
    all_gather x1, blocking collectives, per_device(): all_quads = lax.all_gather(quad_pairs, 'tile', axis=0, tiled=True)  23.3 us
    all_to_all x1, waiting for transfers between devices, per_device(): lax.all_to_all(amp_send, 'tile', split_axis=1, concat_axis=0, tiled=True)  18.8 us
    all_to_all x1, starting transfers between devices, per_device(): lax.all_to_all(amp_send, 'tile', split_axis=1, concat_axis=0, tiled=True)  12.7 us
    all_to_all x1, starting transfers between devices, per_device(): lax.all_to_all(partial_value, 'tile', split_axis=2, concat_axis=0, tiled=...  9.55 us
    reshape x2, local copies, waits for them, and re-layouts, per_device(): cycle.reshape(all_occ, VT, TS, local_occ, VT, TS)  9.15 us
    all_to_all x1, waiting for transfers between devices, per_device(): lax.all_to_all(partial_value, 'tile', split_axis=2, concat_axis=0, tiled=...  8.57 us
    unnamed x9, local copies, waits for them, and re-layouts  7.95 us
    reshape x2, local copies, waits for them, and re-layouts, per_device(): updated.reshape(all_occ, local_occ, VT, VT, TS, TS)  7.69 us
  transfers between devices with their start and end apart: 4, of which 3 were waited for; matrix products, arithmetic and copies ran while one was open for 23% of the time, Pallas kernels for 0%

commit v1 on v0

v1 whole, which is shorter than its diff:
```python
import functools

import jax
import jax.numpy as jnp
from jax import lax
from jax.experimental import pallas as pl
from jax.experimental.pallas import tpu as pltpu
from jax.sharding import PartitionSpec as P

TS = 32
VT = 4
NTP = VT * VT
LANES = 128
GROUPS = LANES // TS
STRIPES = TS // GROUPS


def swap_groups(four):
    lane = lax.broadcasted_iota(jnp.int32, four[0].shape, four[0].ndim - 1)
    low = lane < 2 * TS
    even = (lane // TS) % 2 == 0
    v = list(four)
    for p in (0, 1):
        a, b = v[p], v[p + 2]
        v[p] = jnp.where(low, a, pltpu.roll(b, 2 * TS, 1))
        v[p + 2] = jnp.where(low, pltpu.roll(a, 2 * TS, 1), b)
    for p in (0, 2):
        a, b = v[p], v[p + 1]
        v[p] = jnp.where(even, a, pltpu.roll(b, TS, 1))
        v[p + 1] = jnp.where(even, pltpu.roll(a, LANES - TS, 1), b)
    return v


def finish_kernel(places, targets, part_ref, amp_ref, *rest):
    places, copied = places
    pieces = rest[:copied]
    out_ref, matrix, ladder, columns, product, result, sems = rest[copied:]
    occ = amp_ref.shape[1]
    spread = VT * TS

    copies = []
    for n, piece in enumerate(pieces):
        rows = piece.shape[0]
        start = pl.multiple_of(places[n] * rows, rows)
        copy = pltpu.make_async_copy(piece, matrix.at[pl.ds(start, rows)], sems.at[n])
        copy.start()
        copies.append(copy)

    if part_ref.shape[0] == NTP:
        for q in range(part_ref.shape[0]):
            ladder[targets[q]] = part_ref[q].astype(jnp.float32)
    else:
        ladder[...] = jnp.zeros_like(ladder)
        for q in range(part_ref.shape[0]):
            ladder[targets[q]] += part_ref[q].astype(jnp.float32)

    for C in range(VT):
        for h in range(STRIPES):
            lanes = slice(h * LANES, (h + 1) * LANES)
            four = []
            for B in range(VT):
                pair = C * VT + B
                total = amp_ref[pair, :, lanes].astype(jnp.float32) + ladder[pair, :, lanes]
                four.append(total)
            for g, value in enumerate(swap_groups(four)):
                columns[pl.ds(C * TS + h * GROUPS + g, occ, stride=spread), :] = value
    right = columns[...].astype(jnp.bfloat16)

    for copy in copies:
        copy.wait()
    step = min(512, matrix.shape[0])
    for r in range(0, matrix.shape[0], step):
        product[r:r + step, :] = jnp.dot(
            matrix[r:r + step, :], right, preferred_element_type=jnp.float32
        )

    for A in range(VT):
        for h in range(STRIPES):
            lanes = slice(h * LANES, (h + 1) * LANES)
            four = [
                product[pl.ds(A * TS + h * GROUPS + g, occ, stride=spread), :]
                for g in range(GROUPS)
            ]
            for B, value in enumerate(swap_groups(four)):
                pair = A * VT + B
                result[h, pl.ds(pair, occ, stride=NTP), :] = value + ladder[pair, :, lanes]
    for h in range(STRIPES):
        lanes = slice(h * LANES, (h + 1) * LANES)
        out_ref[:, :, lanes] = result[h].astype(jnp.bfloat16).reshape(occ, NTP, LANES)


def finish(places, targets, part, amp, pieces):
    occ = amp.shape[1]
    rows = occ * VT * TS

    def kernel(places_ref, targets_ref, *refs):
        finish_kernel((places_ref, len(pieces)), targets_ref, *refs)

    whole = pl.BlockSpec(memory_space=pltpu.VMEM)
    scalars = pl.BlockSpec(memory_space=pltpu.SMEM)
    return pl.pallas_call(
        kernel,
        out_shape=jax.ShapeDtypeStruct((occ, NTP, TS * TS), jnp.bfloat16),
        in_specs=[scalars, scalars, whole, whole]
        + [pl.BlockSpec(memory_space=pl.ANY)] * len(pieces),
        out_specs=whole,
        scratch_shapes=[
            pltpu.VMEM((rows, rows), jnp.bfloat16),
            pltpu.VMEM((NTP, occ, TS * TS), jnp.float32),
            pltpu.VMEM((rows, VT * TS), jnp.float32),
            pltpu.VMEM((rows, VT * TS), jnp.float32),
            pltpu.VMEM((STRIPES, occ * NTP, LANES), jnp.float32),
            pltpu.SemaphoreType.DMA((len(pieces),)),
        ],
        compiler_params=pltpu.CompilerParams(vmem_limit_bytes=56 * 1024 * 1024),
        cost_estimate=pl.CostEstimate(
            flops=2 * rows * rows * VT * TS,
            bytes_accessed=2 * rows * rows,
            transcendentals=0,
        ),
    )(places, targets, part, amp, *pieces)


def ladder_kernel(arrived_ref, ints_ref, out_ref, total):
    occ = out_ref.shape[0]
    value = jnp.dot(
        arrived_ref[...].reshape(occ * occ, TS * TS),
        ints_ref[0],
        preferred_element_type=jnp.float32,
    )
    for h in range(STRIPES):
        lanes = slice(h * LANES, (h + 1) * LANES)
        total[h] = value[:, lanes]
        for j in range(occ):
            out_ref[j, :, lanes] = total[h, pl.ds(j, occ, stride=occ), :].astype(jnp.bfloat16)


def ladder_partial(arrived, ladder_ints):
    occ = arrived.shape[0]
    whole = pl.BlockSpec(memory_space=pltpu.VMEM)
    return pl.pallas_call(
        ladder_kernel,
        out_shape=jax.ShapeDtypeStruct((occ, occ, TS * TS), jnp.bfloat16),
        in_specs=[whole, whole],
        out_specs=whole,
        scratch_shapes=[pltpu.VMEM((STRIPES, occ * occ, LANES), jnp.float32)],
        compiler_params=pltpu.CompilerParams(vmem_limit_bytes=40 * 1024 * 1024),
        cost_estimate=pl.CostEstimate(
            flops=2 * occ * occ * TS**4, bytes_accessed=2 * TS**4, transcendentals=0
        ),
    )(arrived, ladder_ints)


def per_device(amps, ladder_ints, quad_pairs, cycle_ints):
    members = lax.axis_size("tile")
    occ = amps.shape[1]
    swap = functools.partial(lax.all_to_all, axis_name="tile", tiled=True)
    matrix = lax.all_gather(cycle_ints, "tile", axis=0, tiled=True)
    tags = jnp.broadcast_to(
        jnp.repeat(quad_pairs.astype(jnp.bfloat16), LANES // 2, axis=1)[:, None, :],
        (occ, NTP, LANES),
    )
    sent = jnp.concatenate([amps[0], tags], axis=2)
    moved = swap(sent, split_axis=0, concat_axis=0)
    pairs = moved[:, 0, TS * TS:].astype(jnp.int32)
    targets, inputs = pairs[:, 0], pairs[:, LANES // 2]
    amp_cycle = moved[:, :, :TS * TS].transpose(1, 0, 2)
    tiles = amps[0].transpose(1, 0, 2)
    wanted = jnp.take(tiles, inputs, axis=0, mode="clip")
    arrived = swap(wanted, split_axis=0, concat_axis=0)
    partial_value = ladder_partial(arrived, ladder_ints)
    part_moved = swap(partial_value, split_axis=0, concat_axis=0)
    residual = finish(jnp.zeros((1,), jnp.int32), targets, part_moved, amp_cycle, [matrix])
    return residual[:, None]


def solution(mesh):
    return jax.shard_map(
        per_device,
        mesh=mesh,
        in_specs=(
            P(("frag", "tile"), None, None, None),
            P(("frag", "tile"), None, None),
            P(("frag", "tile"), None),
            P(("frag", "tile"), None),
        ),
        out_specs=P("frag", "tile", None, None),
        check_vma=False,
    )
```

time: 157 us -> 129 us (0.82)
  blocking collectives: 23.3 us -> 60.1 us
  local copies, waits for them, and re-layouts: 36.2 us -> 4.86 us
  starting transfers between devices: 26.5 us -> 11.2 us
  matrix products: 10.9 us -> 0 us
  other arithmetic: 10.8 us -> 0.12 us
  Pallas kernels: 0 us -> 10.4 us
  waiting for transfers between devices: 34.4 us -> 28 us
    all_to_all x0 -> x2, blocking collectives: none -> 60.1 us  [the longest x1 34.9 us: per_device(): moved = swap(sent, split_axis=0, concat_axis=0)]
    reshape x8 -> x0, local copies, waits for them, and re-layouts: 27.6 us -> none  [the longest x2 9.15 us: per_device(): cycle.reshape(all_occ, VT, TS, local_occ, VT, TS)]
    all_gather x1 -> x0, blocking collectives: 23.3 us -> none  [per_device(): all_quads = lax.all_gather(quad_pairs, 'tile', axis=0, tiled=True)]
    all_to_all x3 -> x1, starting transfers between devices: 26.5 us -> 11.2 us  [per_device(): part_moved = swap(partial_value, split_axis=0, concat_axis=0)]
    all_to_all x3 -> x1, waiting for transfers between devices: 33.7 us -> 21.8 us  [per_device(): part_moved = swap(partial_value, split_axis=0, concat_axis=0)]
    dot_general x3 -> x0, matrix products: 10.9 us -> none  [the longest x1 6.49 us: per_device(): jnp.dot(lax.all_gather(cycle_ints, 'tile', axis=0, tiled=True), cycle_inp...]
    pallas_call x0 -> x2, Pallas kernels: none -> 10.4 us  [the longest x1 8.58 us: finish(): pl.pallas_call(kernel, out_shape=jax.ShapeDtypeStruct((occ, NTP, TS * TS)...]
    all_gather x1, waiting for transfers between devices: 0.01 us -> 5.5 us  [per_device(): matrix = lax.all_gather(cycle_ints, 'tile', axis=0, tiled=True)]
  transfers between devices with their start and end apart: 4 -> 2, of which waited for: 3 -> 2; matrix products, arithmetic and copies ran while one was open for 23% -> 4% of each run, Pallas kernels for 0% -> 1%
where the time goes in v1:
time: 129 us; the launch traced here: 128 us
  blocking collectives  60.1 us (47%)
  waiting for transfers between devices  28 us (22%)
  between operations  13.5 us (10%)
  starting transfers between devices  11.2 us (9%)
  Pallas kernels  10.4 us (8%)
  local copies, waits for them, and re-layouts  4.86 us (4%)
    all_to_all x1, blocking collectives, per_device(): moved = swap(sent, split_axis=0, concat_axis=0)  34.9 us
    all_to_all x1, blocking collectives, per_device(): arrived = swap(wanted, split_axis=0, concat_axis=0)  25.3 us
    all_to_all x1, waiting for transfers between devices, per_device(): part_moved = swap(partial_value, split_axis=0, concat_axis=0)  21.8 us
    all_to_all x1, starting transfers between devices, per_device(): part_moved = swap(partial_value, split_axis=0, concat_axis=0)  11.2 us
    pallas_call x1, Pallas kernels, finish(): pl.pallas_call(kernel, out_shape=jax.ShapeDtypeStruct((occ, NTP, TS * TS)...  8.58 us
    all_gather x1, waiting for transfers between devices, per_device(): matrix = lax.all_gather(cycle_ints, 'tile', axis=0, tiled=True)  5.5 us
  transfers between devices with their start and end apart: 2, of which 2 were waited for; matrix products, arithmetic and copies ran while one was open for 4% of the time, Pallas kernels for 1%

profile of v1, /device:TPU:0, one launch (start us, length us, event | category | flops | bytes accessed | tf_op | source)
XLA Modules:
  0.0 128.2 jit_solution(14147186119375021637)
XLA Ops:
  6.5 0.0 copy-start.2
  6.5 0.0 all-gather.2.cloned.1.call-start
  6.5 0.7 all-gather.2.cloned.1.call-update
  7.3 1.3 %copy.20 = bf16[1,16,16,1024]{3,1,2,0:T(8,128)(2,1)S(1)} copy(bf16[1,16,16,1024]{3,2,1,0:T(8,128)(2,1)} %param.4) | data formatting | bytes 1048576 | tf_op args[0]
  8.6 0.0 copy-done.2
  8.6 0.1 broadcast_in_dim.15
  8.7 0.1 reshape.17
  8.8 0.1 pad_maximum_fusion
  8.9 0.1 copy.12
  9.0 34.9 %all_to_all.15 = bf16[16,16,1152]{2,1,0:T(8,128)(2,1)S(1)} all-to-all(bf16[16,16,1152]{2,1,0:T(8,128)(2,1)S(1)} %copy.12), channel_id=1, replica_groups=mesh['frag'=2,'tile'=16] {'tile'}, dimensions={0} | all-to-all | bytes 1179648 | tf_op jit(solution)/shard_map/all_to_all | solution.py:164
  43.9 0.0 copy-start
  43.9 0.7 slice_reduce_fusion
  44.6 1.4 %gather_fusion = bf16[16,16,1024]{2,1,0:T(8,128)(2,1)} fusion(bf16[16,16,1024]{2,1,0:T(8,128)(2,1)S(1)} %bitcast.16, s32[1024]{0:T(1024)S(1)} %pad_clamp_fusion), kind=kCustom, calls=%fused_computation | custom fusion | bytes 1048640 | tf_op jit(solution)/shard_map/jit(_take)/gather | solution.py:169
  45.9 25.3 %all_to_all.16.arrived_ref = bf16[16,16,1024]{2,1,0:T(8,128)(2,1)S(1)} all-to-all(bf16[16,16,1024]{2,1,0:T(8,128)(2,1)} %gather_fusion), channel_id=1, replica_groups=mesh['frag'=2,'tile'=16] {'tile'}, dimensions={0} | all-to-all | bytes 1048576 | tf_op jit(solution)/shard_map/all_to_all | solution.py:170
  71.2 0.0 copy-done
  71.2 1.8 %shard_map.46 = bf16[16,16,1024]{2,1,0:T(8,128)(2,1)} custom-call(bf16[16,16,1024]{2,1,0:T(8,128)(2,1)S(1)} %all_to_all.16.arrived_ref, bf16[1,1024,1024]{2,1,0:T(8,128)(2,1)S(1)} %copy-done), custom_call_target="tpu_custom_call" | custom-call | flops 536870912 | bytes 2097152 | tf_op jit(solution)/shard_map/pallas_call | solution.py:141
  73.0 11.2 %all-to-all-start.2 = ((bf16[16,16,1024]{2,1,0:T(8,128)(2,1)}), bf16[16,16,1024]{2,1,0:T(8,128)(2,1)S(1)}, u32[]{:S(2)}, u32[]{:S(2)}) async-start(bf16[16,16,1024]{2,1,0:T(8,128)(2,1)} %shard_map.46), calls=%async_computation.2 | async-start | bytes 1048576 | tf_op jit(solution)/shard_map/all_to_all | solution.py:172
  84.2 0.1 slice.21
  84.3 1.1 copy.19
  85.5 21.8 %all-to-all-done.2.refs_0_ = bf16[16,16,1024]{2,1,0:T(8,128)(2,1)S(1)} async-done(((bf16[16,16,1024]{2,1,0:T(8,128)(2,1)}), bf16[16,16,1024]{2,1,0:T(8,128)(2,1)S(1)}, u32[]{:S(2)}, u32[]{:S(2)}) %all-to-all-start.2) | async-done | bytes 524320 | tf_op jit(solution)/shard_map/all_to_all | solution.py:172
  107.3 0.0 copy-start.1
  107.3 5.5 %all-gather.2.cloned.1.call-done.refs_2_ = bf16[2048,2048]{1,0:T(8,128)(2,1)} async-done(((bf16[128,2048]{1,0:T(8,128)(2,1)}), bf16[2048,2048]{1,0:T(8,128)(2,1)}) %all-gather.2.cloned.1.call-update) | async-done | bytes 8388624 | tf_op jit(solution)/shard_map/all_gather | solution.py:158
  112.8 0.0 copy-done.1
  112.8 8.6 %shard_map.47 = bf16[16,16,1024]{2,1,0:T(8,128)(2,1)} custom-call(s32[1]{0:T(128)} %constant.0.clone.1.places_ref, s32[16]{0:T(128)} %get-tuple-element.6.targets_ref, bf16[16,16,1024]{2,1,0:T(8,128)(2,1)} %copy-done.1, bf16[16,16,1024]{2,1,0:T(8,128)(2,1)} %bitcast.17, bf16[2048,2048]{1,0:T(8,128)(2,1)} %all-gather.2.cloned.1.call-done.refs_2_), custom_call_target="tpu_custom_call" | custom-call | flops 1073741824 | bytes 8388608 | tf_op jit(solution)/shard_map/pallas_call | solution.py:101
  (4 shorter events, 0.0 us)
Async XLA Ops:
  6.5 2.1 %copy-start.2 = (s32[1,2]{1,0:T(1,128)S(1)}, s32[1,2]{1,0:T(1,128)}, u32[]{:S(2)}) copy-start(s32[1,2]{1,0:T(1,128)} %param.6) | copy-start | bytes 28
  6.5 106.2 %all-gather.2.cloned.1.call-start = ((), (), s32[]{:S(2)}) async-start(), calls=%async_computation.3 | async-start | bytes 8912896 | tf_op jit(solution)/shard_map/all_gather | solution.py:158
  43.9 27.3 %copy-start = (bf16[1,1024,1024]{2,1,0:T(8,128)(2,1)S(1)}, bf16[1,1024,1024]{2,1,0:T(8,128)(2,1)}, u32[]{:S(2)}) copy-start(bf16[1,1024,1024]{2,1,0:T(8,128)(2,1)} %ints_ref.1) | copy-start | bytes 6291460
  73.0 34.2 %all-to-all-start.2 = ((bf16[16,16,1024]{2,1,0:T(8,128)(2,1)}), bf16[16,16,1024]{2,1,0:T(8,128)(2,1)S(1)}, u32[]{:S(2)}, u32[]{:S(2)}) async-start(bf16[16,16,1024]{2,1,0:T(8,128)(2,1)} %shard_map.46), calls=%async_computation.2 | async-start | bytes 1048576 | tf_op jit(solution)/shard_map/all_to_all | solution.py:172
  107.3 5.5 %copy-start.1 = (bf16[16,16,1024]{2,1,0:T(8,128)(2,1)}, bf16[16,16,1024]{2,1,0:T(8,128)(2,1)S(1)}, u32[]{:S(2)}) copy-start(bf16[16,16,1024]{2,1,0:T(8,128)(2,1)S(1)} %all-to-all-done.2.refs_0_) | copy-start | bytes 1572868
Sparse Core Ops, SparseCore 0:
  9.5 103.1 all-gather.1

commit v2 on v1

--- a/solution.py
+++ b/solution.py
@@ -2,6 +2,7 @@
 
 import jax
 import jax.numpy as jnp
+import numpy as np
 from jax import lax
 from jax.experimental import pallas as pl
 from jax.experimental.pallas import tpu as pltpu
@@ -13,6 +14,8 @@
 LANES = 128
 GROUPS = LANES // TS
 STRIPES = TS // GROUPS
+SIDES = 2
+CORES = 2
 
 
 def swap_groups(four):
@@ -34,17 +37,9 @@
 def finish_kernel(places, targets, part_ref, amp_ref, *rest):
     places, copied = places
     pieces = rest[:copied]
-    out_ref, matrix, ladder, columns, product, result, sems = rest[copied:]
+    out_ref, ladder, columns, product, result = rest[copied:]
     occ = amp_ref.shape[1]
     spread = VT * TS
-
-    copies = []
-    for n, piece in enumerate(pieces):
-        rows = piece.shape[0]
-        start = pl.multiple_of(places[n] * rows, rows)
-        copy = pltpu.make_async_copy(piece, matrix.at[pl.ds(start, rows)], sems.at[n])
-        copy.start()
-        copies.append(copy)
 
     if part_ref.shape[0] == NTP:
         for q in range(part_ref.shape[0]):
@@ -66,12 +61,11 @@
                 columns[pl.ds(C * TS + h * GROUPS + g, occ, stride=spread), :] = value
     right = columns[...].astype(jnp.bfloat16)
 
-    for copy in copies:
-        copy.wait()
-    step = min(512, matrix.shape[0])
-    for r in range(0, matrix.shape[0], step):
-        product[r:r + step, :] = jnp.dot(
-            matrix[r:r + step, :], right, preferred_element_type=jnp.float32
+    for n, piece in enumerate(pieces):
+        rows = piece.shape[0]
+        start = pl.multiple_of(places[n] * rows, rows)
+        product[pl.ds(start, rows), :] = jnp.dot(
+            piece[...], right, preferred_element_type=jnp.float32
         )
 
     for A in range(VT):
@@ -101,18 +95,17 @@
     return pl.pallas_call(
         kernel,
         out_shape=jax.ShapeDtypeStruct((occ, NTP, TS * TS), jnp.bfloat16),
-        in_specs=[scalars, scalars, whole, whole]
-        + [pl.BlockSpec(memory_space=pl.ANY)] * len(pieces),
+        in_specs=[scalars, scalars] + [whole] * (2 + len(pieces)),
         out_specs=whole,
         scratch_shapes=[
-            pltpu.VMEM((rows, rows), jnp.bfloat16),
             pltpu.VMEM((NTP, occ, TS * TS), jnp.float32),
             pltpu.VMEM((rows, VT * TS), jnp.float32),
             pltpu.VMEM((rows, VT * TS), jnp.float32),
             pltpu.VMEM((STRIPES, occ * NTP, LANES), jnp.float32),
-            pltpu.SemaphoreType.DMA((len(pieces),)),
         ],
-        compiler_params=pltpu.CompilerParams(vmem_limit_bytes=56 * 1024 * 1024),
+        compiler_params=pltpu.CompilerParams(
+            vmem_limit_bytes=2 * rows * rows + (rows // 128) * 1024 * 1024
+        ),
         cost_estimate=pl.CostEstimate(
             flops=2 * rows * rows * VT * TS,
             bytes_accessed=2 * rows * rows,
@@ -144,33 +137,113 @@
         in_specs=[whole, whole],
         out_specs=whole,
         scratch_shapes=[pltpu.VMEM((STRIPES, occ * occ, LANES), jnp.float32)],
-        compiler_params=pltpu.CompilerParams(vmem_limit_bytes=40 * 1024 * 1024),
+        compiler_params=pltpu.CompilerParams(vmem_limit_bytes=20 * 1024 * 1024),
         cost_estimate=pl.CostEstimate(
             flops=2 * occ * occ * TS**4, bytes_accessed=2 * TS**4, transcendentals=0
         ),
     )(arrived, ladder_ints)
+
+
+def routes(members):
+    lines = members // (SIDES * CORES)
+    ring = list(range(0, lines, 2)) + list(range(1, lines, 2))[::-1]
+    place = {line: n for n, line in enumerate(ring)}
+
+    def member(line, side, core):
+        return (line * SIDES + side) * CORES + core
+
+    def split(t):
+        return t // (SIDES * CORES), t // CORES % SIDES, t % CORES
+
+    def behind(t, step):
+        line, side, core = split(t)
+        back = step if core == 0 else -step
+        return member(ring[(place[line] - back) % lines], side, core)
+
+    def across(t):
+        line, side, core = split(t)
+        return member(line, (side + 1) % SIDES, core)
+
+    def beside(t):
+        line, side, core = split(t)
+        return member(line, side, (core + 1) % CORES)
+
+    every = range(members)
+    moves = {
+        "ahead": [(behind(t, 1), t) for t in every],
+        "back": [(behind(t, -1), t) for t in every],
+        "over": [(across(t), t) for t in every],
+        "pair": [(beside(t), t) for t in every],
+    }
+    return moves, {"ahead": lambda t: behind(t, 1), "back": lambda t: behind(t, -1), "over": across, "pair": beside}
+
+
+class Gather:
+    def __init__(self, block, members):
+        self.members = members
+        self.lines = members // (SIDES * CORES)
+        self.moves, self.source = routes(members)
+        self.blocks = [(block, list(range(members)), ("ahead", "back", "over", "pair"), 0)]
+        self.fresh = list(self.blocks)
+
+    def move(self, item, kind):
+        block, owners, _, hops = item
+        source = self.source[kind]
+        new_owners = [owners[source(t)] for t in range(self.members)]
+        follow = {"ahead": ("ahead", "over", "pair"), "back": ("back", "over", "pair"), "over": ("pair",), "pair": ()}[kind]
+        hops = hops + 1 if kind in ("ahead", "back") else hops
+        limit = {"ahead": self.lines // 2, "back": (self.lines - 1) // 2}
+        follow = tuple(k for k in follow if hops < limit.get(k, hops + 1))
+        return lax.ppermute(block, "tile", self.moves[kind]), new_owners, follow, hops
+
+    def round(self):
+        new = []
+        for kind in ("ahead", "back", "over", "pair"):
+            for item in self.fresh:
+                if kind in item[2]:
+                    new.append(self.move(item, kind))
+        self.blocks += new
+        self.fresh = new
+
+    def tie(self, value):
+        held = [item[0] for item in self.fresh]
+        value, held = lax.optimization_barrier((value, held))
+        tied = [(block,) + item[1:] for block, item in zip(held, self.fresh)]
+        self.blocks[len(self.blocks) - len(tied):] = tied
+        self.fresh = tied
+        return value
+
+    def places(self):
+        table = np.array([item[1] for item in self.blocks], np.int32).T
+        return lax.dynamic_index_in_dim(jnp.asarray(table), lax.axis_index("tile"), 0, keepdims=False)
 
 
 def per_device(amps, ladder_ints, quad_pairs, cycle_ints):
     members = lax.axis_size("tile")
     occ = amps.shape[1]
     swap = functools.partial(lax.all_to_all, axis_name="tile", tiled=True)
-    matrix = lax.all_gather(cycle_ints, "tile", axis=0, tiled=True)
+    rows = Gather(cycle_ints, members)
     tags = jnp.broadcast_to(
         jnp.repeat(quad_pairs.astype(jnp.bfloat16), LANES // 2, axis=1)[:, None, :],
         (occ, NTP, LANES),
     )
     sent = jnp.concatenate([amps[0], tags], axis=2)
-    moved = swap(sent, split_axis=0, concat_axis=0)
+    rows.round()
+    moved = rows.tie(swap(sent, split_axis=0, concat_axis=0))
     pairs = moved[:, 0, TS * TS:].astype(jnp.int32)
     targets, inputs = pairs[:, 0], pairs[:, LANES // 2]
     amp_cycle = moved[:, :, :TS * TS].transpose(1, 0, 2)
     tiles = amps[0].transpose(1, 0, 2)
     wanted = jnp.take(tiles, inputs, axis=0, mode="clip")
-    arrived = swap(wanted, split_axis=0, concat_axis=0)
+    rows.round()
+    arrived = rows.tie(swap(wanted, split_axis=0, concat_axis=0))
     partial_value = ladder_partial(arrived, ladder_ints)
-    part_moved = swap(partial_value, split_axis=0, concat_axis=0)
-    residual = finish(jnp.zeros((1,), jnp.int32), targets, part_moved, amp_cycle, [matrix])
+    rows.round()
+    part_moved = rows.tie(swap(partial_value, split_axis=0, concat_axis=0))
+    while rows.fresh:
+        rows.round()
+    pieces = [item[0] for item in rows.blocks]
+    residual = finish(rows.places(), targets, part_moved, amp_cycle, pieces)
     return residual[:, None]
 
 

time: 129 us -> 134 us (1.039)
  blocking collectives: 60.1 us -> 0 us
  waiting for transfers between devices: 28 us -> 74 us
  starting transfers between devices: 11.2 us -> 28.5 us
  local copies, waits for them, and re-layouts: 4.86 us -> 19.6 us
  between operations: 13.5 us -> 0.19 us
  Pallas kernels: 10.4 us -> 8.87 us
  other arithmetic: 0.12 us -> 1.53 us
    ppermute x0 -> x15, waiting for transfers between devices: none -> 74 us  [move(): lax.ppermute(block, 'tile', self.moves[kind])]
    all_to_all x2 -> x0, blocking collectives: 60.1 us -> none  [the longest x1 34.9 us: per_device(): moved = swap(sent, split_axis=0, concat_axis=0)]
    all_to_all x1 -> x3, waiting for transfers between devices: 21.8 us -> 0.01 us  [the longest x1 0.01 us: per_device(): arrived = rows.tie(swap(wanted, split_axis=0, concat_axis=0))]
    ppermute x0 -> x15, starting transfers between devices: none -> 12.7 us  [move(): lax.ppermute(block, 'tile', self.moves[kind])]
    unnamed x8 -> x45, local copies, waits for them, and re-layouts: 2.49 us -> 15 us
    all_gather x1 -> x0, waiting for transfers between devices: 5.5 us -> none  [per_device(): matrix = lax.all_gather(cycle_ints, 'tile', axis=0, tiled=True)]
    all_to_all x1 -> x3, starting transfers between devices: 11.2 us -> 15.9 us  [the longest x1 7.43 us: per_device(): moved = rows.tie(swap(sent, split_axis=0, concat_axis=0))]
    pallas_call x1, Pallas kernels: 8.58 us -> 7.07 us  [finish(): pl.pallas_call(kernel, out_shape=jax.ShapeDtypeStruct((occ, NTP, TS * TS)...]
  transfers between devices with their start and end apart: 2 -> 18, of which waited for: 2 -> 6; matrix products, arithmetic and copies ran while one was open for 4% -> 2% of each run, Pallas kernels for 1% -> 0%
where the time goes in v2:
time: 134 us; the launch traced here: 133 us
  waiting for transfers between devices  74 us (55%)
  starting transfers between devices  28.5 us (21%)
  local copies, waits for them, and re-layouts  19.6 us (15%)
  Pallas kernels  8.87 us (7%)
  other arithmetic  1.53 us (1%)
    ppermute x15, waiting for transfers between devices, move(): lax.ppermute(block, 'tile', self.moves[kind])  74 us
    unnamed x45, local copies, waits for them, and re-layouts  15 us
    ppermute x15, starting transfers between devices, move(): lax.ppermute(block, 'tile', self.moves[kind])  12.7 us
    all_to_all x1, starting transfers between devices, per_device(): moved = rows.tie(swap(sent, split_axis=0, concat_axis=0))  7.43 us
    pallas_call x1, Pallas kernels, finish(): pl.pallas_call(kernel, out_shape=jax.ShapeDtypeStruct((occ, NTP, TS * TS)...  7.07 us
    all_to_all x1, starting transfers between devices, per_device(): part_moved = rows.tie(swap(partial_value, split_axis=0, concat_axis=0))  4.65 us
    all_to_all x1, starting transfers between devices, per_device(): arrived = rows.tie(swap(wanted, split_axis=0, concat_axis=0))  3.78 us
  transfers between devices with their start and end apart: 18, of which 6 were waited for; matrix products, arithmetic and copies ran while one was open for 2% of the time, Pallas kernels for 0%

profile of v2, /device:TPU:0, one launch (start us, length us, event | category | flops | bytes accessed | tf_op | source)
XLA Modules:
  0.0 132.7 jit_solution(3057701467779614168)
XLA Ops:
  0.0 0.7 convert_bitcast_fusion
  0.7 0.1 broadcast_in_dim.15
  0.7 0.1 reshape.17
  0.8 1.3 %copy.18 = bf16[1,16,16,1024]{3,1,2,0:T(8,128)(2,1)S(1)} copy(bf16[1,16,16,1024]{3,2,1,0:T(8,128)(2,1)} %param.5) | data formatting | bytes 1048576 | tf_op args[0]
  2.2 0.1 pad_maximum_fusion
  2.3 1.0 copy.13
  3.2 7.4 %all-to-all-start = ((bf16[16,16,1152]{2,1,0:T(8,128)(2,1)}), bf16[16,16,1152]{2,1,0:T(8,128)(2,1)}, u32[]{:S(2)}, u32[]{:S(2)}) async-start(bf16[16,16,1152]{2,1,0:T(8,128)(2,1)} %copy.13), calls=%async_computation | async-start | bytes 1179648 | tf_op jit(solution)/shard_map/all_to_all | solution.py:232
  10.7 1.9 %collective-permute-start.2 = (bf16[128,2048]{1,0:T(8,128)(2,1)S(1)}, bf16[128,2048]{1,0:T(8,128)(2,1)}, u32[]{:S(2)}, u32[]{:S(2)}) collective-permute-start(bf16[128,2048]{1,0:T(8,128)(2,1)S(1)} %copy-done.1), channel_id=1, source_target_pairs={{2,0},{3,1},{0,2},{1,3},{6,4},{7,5},{4,6},{5,7},{10,8},{11,9},{8,1... | collective-permute-start | bytes 1572872 | tf_op jit(solution)/shard_map/ppermute | solution.py:197
  12.6 1.5 %collective-permute-start.1 = (bf16[128,2048]{1,0:T(8,128)(2,1)S(1)}, bf16[128,2048]{1,0:T(8,128)(2,1)S(1)}, u32[]{:S(2)}, u32[]{:S(2)}) collective-permute-start(bf16[128,2048]{1,0:T(8,128)(2,1)S(1)} %copy-done.1), channel_id=1, source_target_pairs={{8,0},{5,1},{10,2},{7,3},{0,4},{13,5},{2,6},{15,7},{12,8},{1,9},{1... | collective-permute-start | bytes 1572872 | tf_op jit(solution)/shard_map/ppermute | solution.py:197
  14.1 1.5 %collective-permute-start = (bf16[128,2048]{1,0:T(8,128)(2,1)S(1)}, bf16[128,2048]{1,0:T(8,128)(2,1)S(1)}, u32[]{:S(2)}, u32[]{:S(2)}) collective-permute-start(bf16[128,2048]{1,0:T(8,128)(2,1)S(1)} %copy-done.1), channel_id=1, source_target_pairs={{4,0},{9,1},{6,2},{11,3},{12,4},{1,5},{14,6},{3,7},{0,8},{13,9},{2... | collective-permute-start | bytes 1572872 | tf_op jit(solution)/shard_map/ppermute | solution.py:197
  15.6 15.9 %collective-permute-done.2.refs_5_ = bf16[128,2048]{1,0:T(8,128)(2,1)} collective-permute-done((bf16[128,2048]{1,0:T(8,128)(2,1)S(1)}, bf16[128,2048]{1,0:T(8,128)(2,1)}, u32[]{:S(2)}, u32[]{:S(2)}) %collective-permute-start.2) | collective-permute-done | bytes 524320 | tf_op jit(solution)/shard_map/ppermute | solution.py:197
  31.4 18.4 %collective-permute-done.1.refs_4_ = bf16[128,2048]{1,0:T(8,128)(2,1)S(1)} collective-permute-done((bf16[128,2048]{1,0:T(8,128)(2,1)S(1)}, bf16[128,2048]{1,0:T(8,128)(2,1)S(1)}, u32[]{:S(2)}, u32[]{:S(2)}) %collective-permute-start.1) | collective-permute-done | bytes 524320 | tf_op jit(solution)/shard_map/ppermute | solution.py:197
  49.8 0.8 copy-done.2
  50.6 0.8 copy-done.4
  51.4 0.8 copy-done.6
  52.2 0.8 slice_convert_fusion
  53.0 0.2 slice_reduce_fusion
  53.3 1.4 %gather_fusion = bf16[16,16,1024]{2,1,0:T(8,128)(2,1)} fusion(bf16[16,16,1024]{2,1,0:T(8,128)(2,1)S(1)} %bitcast.17, s32[1024]{0:T(1024)S(1)} %pad_clamp_fusion), kind=kCustom, calls=%fused_computation | custom fusion | bytes 1048640 | tf_op jit(solution)/shard_map/jit(_take)/gather | solution.py:237
  54.7 3.8 %all-to-all-start.1 = ((bf16[16,16,1024]{2,1,0:T(8,128)(2,1)}), bf16[16,16,1024]{2,1,0:T(8,128)(2,1)S(1)}, u32[]{:S(2)}, u32[]{:S(2)}) async-start(bf16[16,16,1024]{2,1,0:T(8,128)(2,1)} %gather_fusion), calls=%async_computation.1 | async-start | bytes 1048576 | tf_op jit(solution)/shard_map/all_to_all | solution.py:239
  58.5 0.4 collective-permute-start.8
  58.9 1.7 %collective-permute-start.6 = (bf16[128,2048]{1,0:T(8,128)(2,1)}, bf16[128,2048]{1,0:T(8,128)(2,1)S(1)}, u32[]{:S(2)}, u32[]{:S(2)}) collective-permute-start(bf16[128,2048]{1,0:T(8,128)(2,1)} %copy-done.2), channel_id=1, source_target_pairs={{2,0},{3,1},{0,2},{1,3},{6,4},{7,5},{4,6},{5,7},{10,8},{11,9},{8,1... | collective-permute-start | bytes 1572872 | tf_op jit(solution)/shard_map/ppermute | solution.py:197
  60.6 0.3 collective-permute-start.5
  60.9 2.6 %collective-permute-start.4 = (bf16[128,2048]{1,0:T(8,128)(2,1)}, bf16[128,2048]{1,0:T(8,128)(2,1)}, u32[]{:S(2)}, u32[]{:S(2)}) collective-permute-start(bf16[128,2048]{1,0:T(8,128)(2,1)} %copy-done.4), channel_id=1, source_target_pairs={{4,0},{9,1},{6,2},{11,3},{12,4},{1,5},{14,6},{3,7},{0,8},{13,9},{2... | collective-permute-start | bytes 1572872 | tf_op jit(solution)/shard_map/ppermute | solution.py:197
  63.5 0.8 copy-done.8
  64.3 14.6 %collective-permute-done.6.refs_9_ = bf16[128,2048]{1,0:T(8,128)(2,1)S(1)} collective-permute-done((bf16[128,2048]{1,0:T(8,128)(2,1)}, bf16[128,2048]{1,0:T(8,128)(2,1)S(1)}, u32[]{:S(2)}, u32[]{:S(2)}) %collective-permute-start.6) | collective-permute-done | bytes 524320 | tf_op jit(solution)/shard_map/ppermute | solution.py:197
  78.9 0.8 copy-done.12
  79.8 9.9 %collective-permute-done.5.refs_8_ = bf16[128,2048]{1,0:T(8,128)(2,1)S(1)} collective-permute-done((bf16[128,2048]{1,0:T(8,128)(2,1)}, bf16[128,2048]{1,0:T(8,128)(2,1)S(1)}, u32[]{:S(2)}, u32[]{:S(2)}) %collective-permute-start.5) | collective-permute-done | bytes 524320 | tf_op jit(solution)/shard_map/ppermute | solution.py:197
  89.7 0.8 copy-done.14
  90.5 1.8 %shard_map.55 = bf16[16,16,1024]{2,1,0:T(8,128)(2,1)} custom-call(bf16[16,16,1024]{2,1,0:T(8,128)(2,1)S(1)} %all-to-all-done.1.arrived_ref, bf16[1,1024,1024]{2,1,0:T(8,128)(2,1)S(1)} %copy-done), custom_call_target="tpu_custom_call" | custom-call | flops 536870912 | bytes 2097152 | tf_op jit(solution)/shard_map/pallas_call | solution.py:134
  92.3 4.6 %all-to-all-start.2 = ((bf16[16,16,1024]{2,1,0:T(8,128)(2,1)}), bf16[16,16,1024]{2,1,0:T(8,128)(2,1)S(1)}, u32[]{:S(2)}, u32[]{:S(2)}) async-start(bf16[16,16,1024]{2,1,0:T(8,128)(2,1)} %shard_map.55), calls=%async_computation.2 | async-start | bytes 1048576 | tf_op jit(solution)/shard_map/all_to_all | solution.py:242
  97.0 0.5 collective-permute-start.12
  97.5 0.1 collective-permute-start.13
  97.6 0.4 collective-permute-start.11
  98.0 1.7 %collective-permute-start.10 = (bf16[128,2048]{1,0:T(8,128)(2,1)}, bf16[128,2048]{1,0:T(8,128)(2,1)}, u32[]{:S(2)}, u32[]{:S(2)}) collective-permute-start(bf16[128,2048]{1,0:T(8,128)(2,1)} %collective-permute-done.4.refs_7_), channel_id=1, source_target_pairs={{2,0},{3,1},{0,2},{1,3},{6,4},{7,5},{4,6},{5,7},{10,8},{11,9},{8,1... | collective-permute-start | bytes 1572872 | tf_op jit(solution)/shard_map/ppermute | solution.py:197
  99.7 0.9 copy-done.16
  100.5 0.8 copy-done.18
  101.4 0.8 copy-done.20
  102.2 14.9 %collective-permute-done.10.refs_13_ = bf16[128,2048]{1,0:T(8,128)(2,1)} collective-permute-done((bf16[128,2048]{1,0:T(8,128)(2,1)}, bf16[128,2048]{1,0:T(8,128)(2,1)}, u32[]{:S(2)}, u32[]{:S(2)}) %collective-permute-start.10) | collective-permute-done | bytes 524320 | tf_op jit(solution)/shard_map/ppermute | solution.py:197
  117.1 0.7 dynamic-slice_bitcast_fusion.places_ref
  117.8 1.2 copy.14
  119.0 0.3 collective-permute-done.14.refs_17_
  119.4 1.0 copy-done.11
  120.4 1.0 copy-done.13
  121.4 1.0 copy-done.15
  122.5 1.0 copy-done.17
  123.5 1.0 copy-done.19
  124.6 1.0 copy-done.21
  125.6 7.1 %shard_map.56 = bf16[16,16,1024]{2,1,0:T(8,128)(2,1)} custom-call(s32[16]{0:T(128)S(1)} %dynamic-slice_bitcast_fusion.places_ref, s32[16]{0:T(128)S(1)} %get-tuple-element.40.targets_ref, bf16[16,16,1024]{2,1,0:T(8,128)(2,1)S(1)} %all-to-all-done.2.refs_0_, bf16[16,16,1024]{2,1,0:T(8,128)(2,1)S(1)} %slice_bitcast_fusion.refs_1_, ...), custom_call_target="tpu_custom_call" | custom-call | flops 1073741824 | bytes 8388608 | tf_op jit(solution)/shard_map/pallas_call | solution.py:95
  (48 shorter events, 0.3 us)
Async XLA Ops:
  2.3 8.4 %copy-start.1 = (bf16[128,2048]{1,0:T(8,128)(2,1)S(1)}, bf16[128,2048]{1,0:T(8,128)(2,1)}, u32[]{:S(2)}) copy-start(bf16[128,2048]{1,0:T(8,128)(2,1)} %refs_2_.1) | copy-start | bytes 1572868
  3.2 49.0 %all-to-all-start = ((bf16[16,16,1152]{2,1,0:T(8,128)(2,1)}), bf16[16,16,1152]{2,1,0:T(8,128)(2,1)}, u32[]{:S(2)}, u32[]{:S(2)}) async-start(bf16[16,16,1152]{2,1,0:T(8,128)(2,1)} %copy.13), calls=%async_computation | async-start | bytes 1179648 | tf_op jit(solution)/shard_map/all_to_all | solution.py:232
  10.7 79.8 %copy-start = (bf16[1,1024,1024]{2,1,0:T(8,128)(2,1)S(1)}, bf16[1,1024,1024]{2,1,0:T(8,128)(2,1)}, u32[]{:S(2)}) copy-start(bf16[1,1024,1024]{2,1,0:T(8,128)(2,1)} %ints_ref.1) | copy-start | bytes 6291460
  10.7 20.7 %collective-permute-start.2 = (bf16[128,2048]{1,0:T(8,128)(2,1)S(1)}, bf16[128,2048]{1,0:T(8,128)(2,1)}, u32[]{:S(2)}, u32[]{:S(2)}) collective-permute-start(bf16[128,2048]{1,0:T(8,128)(2,1)S(1)} %copy-done.1), channel_id=1, source_target_pairs={{2,0},{3,1},{0,2},{1,3},{6,4},{7,5},{4,6},{5,7},{10,8},{11,9},{8,1... | collective-permute-start | bytes 1572872 | tf_op jit(solution)/shard_map/ppermute | solution.py:197
  12.6 37.2 %collective-permute-start.1 = (bf16[128,2048]{1,0:T(8,128)(2,1)S(1)}, bf16[128,2048]{1,0:T(8,128)(2,1)S(1)}, u32[]{:S(2)}, u32[]{:S(2)}) collective-permute-start(bf16[128,2048]{1,0:T(8,128)(2,1)S(1)} %copy-done.1), channel_id=1, source_target_pairs={{8,0},{5,1},{10,2},{7,3},{0,4},{13,5},{2,6},{15,7},{12,8},{1,9},{1... | collective-permute-start | bytes 1572872 | tf_op jit(solution)/shard_map/ppermute | solution.py:197
  14.1 35.7 %collective-permute-start = (bf16[128,2048]{1,0:T(8,128)(2,1)S(1)}, bf16[128,2048]{1,0:T(8,128)(2,1)S(1)}, u32[]{:S(2)}, u32[]{:S(2)}) collective-permute-start(bf16[128,2048]{1,0:T(8,128)(2,1)S(1)} %copy-done.1), channel_id=1, source_target_pairs={{4,0},{9,1},{6,2},{11,3},{12,4},{1,5},{14,6},{3,7},{0,8},{13,9},{2... | collective-permute-start | bytes 1572872 | tf_op jit(solution)/shard_map/ppermute | solution.py:197
  15.6 35.9 %collective-permute-start.3 = (bf16[128,2048]{1,0:T(8,128)(2,1)S(1)}, bf16[128,2048]{1,0:T(8,128)(2,1)S(1)}, u32[]{:S(2)}, u32[]{:S(2)}) collective-permute-start(bf16[128,2048]{1,0:T(8,128)(2,1)S(1)} %copy-done.1), channel_id=1, source_target_pairs={{1,0},{0,1},{3,2},{2,3},{5,4},{4,5},{7,6},{6,7},{9,8},{8,9},{11,10... | collective-permute-start | bytes 1572872 | tf_op jit(solution)/shard_map/ppermute | solution.py:197
  49.8 0.8 copy-start.2
  50.6 0.8 copy-start.4
  51.4 0.8 copy-start.6
  53.2 7.7 %collective-permute-start.9 = (bf16[128,2048]{1,0:T(8,128)(2,1)}, bf16[128,2048]{1,0:T(8,128)(2,1)}, u32[]{:S(2)}, u32[]{:S(2)}) collective-permute-start(bf16[128,2048]{1,0:T(8,128)(2,1)} %collective-permute-done.2.refs_5_), channel_id=1, source_target_pairs={{1,0},{0,1},{3,2},{2,3},{5,4},{4,5},{7,6},{6,7},{9,8},{8,9},{11,10... | collective-permute-start | bytes 1572872 | tf_op jit(solution)/shard_map/ppermute | solution.py:197
  54.7 35.9 %all-to-all-start.1 = ((bf16[16,16,1024]{2,1,0:T(8,128)(2,1)}), bf16[16,16,1024]{2,1,0:T(8,128)(2,1)S(1)}, u32[]{:S(2)}, u32[]{:S(2)}) async-start(bf16[16,16,1024]{2,1,0:T(8,128)(2,1)} %gather_fusion), calls=%async_computation.1 | async-start | bytes 1048576 | tf_op jit(solution)/shard_map/all_to_all | solution.py:239
  58.5 5.1 %collective-permute-start.8 = (bf16[128,2048]{1,0:T(8,128)(2,1)}, bf16[128,2048]{1,0:T(8,128)(2,1)S(1)}, u32[]{:S(2)}, u32[]{:S(2)}) collective-permute-start(bf16[128,2048]{1,0:T(8,128)(2,1)} %copy-done.2), channel_id=1, source_target_pairs={{1,0},{0,1},{3,2},{2,3},{5,4},{4,5},{7,6},{6,7},{9,8},{8,9},{11,10... | collective-permute-start | bytes 1572872 | tf_op jit(solution)/shard_map/ppermute | solution.py:197
  58.9 20.0 %collective-permute-start.6 = (bf16[128,2048]{1,0:T(8,128)(2,1)}, bf16[128,2048]{1,0:T(8,128)(2,1)S(1)}, u32[]{:S(2)}, u32[]{:S(2)}) collective-permute-start(bf16[128,2048]{1,0:T(8,128)(2,1)} %copy-done.2), channel_id=1, source_target_pairs={{2,0},{3,1},{0,2},{1,3},{6,4},{7,5},{4,6},{5,7},{10,8},{11,9},{8,1... | collective-permute-start | bytes 1572872 | tf_op jit(solution)/shard_map/ppermute | solution.py:197
  60.5 18.4 %collective-permute-start.7 = (bf16[128,2048]{1,0:T(8,128)(2,1)}, bf16[128,2048]{1,0:T(8,128)(2,1)S(1)}, u32[]{:S(2)}, u32[]{:S(2)}) collective-permute-start(bf16[128,2048]{1,0:T(8,128)(2,1)} %copy-done.4), channel_id=1, source_target_pairs={{1,0},{0,1},{3,2},{2,3},{5,4},{4,5},{7,6},{6,7},{9,8},{8,9},{11,10... | collective-permute-start | bytes 1572872 | tf_op jit(solution)/shard_map/ppermute | solution.py:197
  60.6 29.1 %collective-permute-start.5 = (bf16[128,2048]{1,0:T(8,128)(2,1)}, bf16[128,2048]{1,0:T(8,128)(2,1)S(1)}, u32[]{:S(2)}, u32[]{:S(2)}) collective-permute-start(bf16[128,2048]{1,0:T(8,128)(2,1)} %copy-done.4), channel_id=1, source_target_pairs={{2,0},{3,1},{0,2},{1,3},{6,4},{7,5},{4,6},{5,7},{10,8},{11,9},{8,1... | collective-permute-start | bytes 1572872 | tf_op jit(solution)/shard_map/ppermute | solution.py:197
  60.9 29.6 %collective-permute-start.4 = (bf16[128,2048]{1,0:T(8,128)(2,1)}, bf16[128,2048]{1,0:T(8,128)(2,1)}, u32[]{:S(2)}, u32[]{:S(2)}) collective-permute-start(bf16[128,2048]{1,0:T(8,128)(2,1)} %copy-done.4), channel_id=1, source_target_pairs={{4,0},{9,1},{6,2},{11,3},{12,4},{1,5},{14,6},{3,7},{0,8},{13,9},{2... | collective-permute-start | bytes 1572872 | tf_op jit(solution)/shard_map/ppermute | solution.py:197
  63.5 0.8 copy-start.8
  78.9 10.8 %copy-start.10 = (bf16[128,2048]{1,0:T(8,128)(2,1)}, bf16[128,2048]{1,0:T(8,128)(2,1)S(1)}, u32[]{:S(2)}) copy-start(bf16[128,2048]{1,0:T(8,128)(2,1)S(1)} %collective-permute-done.6.refs_9_) | copy-start | bytes 1572868
  78.9 0.8 copy-start.12
  89.7 0.8 copy-start.14
  92.3 24.7 %all-to-all-start.2 = ((bf16[16,16,1024]{2,1,0:T(8,128)(2,1)}), bf16[16,16,1024]{2,1,0:T(8,128)(2,1)S(1)}, u32[]{:S(2)}, u32[]{:S(2)}) async-start(bf16[16,16,1024]{2,1,0:T(8,128)(2,1)} %shard_map.55), calls=%async_computation.2 | async-start | bytes 1048576 | tf_op jit(solution)/shard_map/all_to_all | solution.py:242
  97.0 22.3 %copy-start.3 = (bf16[128,2048]{1,0:T(8,128)(2,1)S(1)}, bf16[128,2048]{1,0:T(8,128)(2,1)}, u32[]{:S(2)}) copy-start(bf16[128,2048]{1,0:T(8,128)(2,1)} %copy-done.2) | copy-start | bytes 1572868
  97.0 22.3 %copy-start.5 = (bf16[128,2048]{1,0:T(8,128)(2,1)S(1)}, bf16[128,2048]{1,0:T(8,128)(2,1)}, u32[]{:S(2)}) copy-start(bf16[128,2048]{1,0:T(8,128)(2,1)} %copy-done.4) | copy-start | bytes 1572868
  97.0 22.3 %copy-start.7 = (bf16[128,2048]{1,0:T(8,128)(2,1)S(1)}, bf16[128,2048]{1,0:T(8,128)(2,1)}, u32[]{:S(2)}) copy-start(bf16[128,2048]{1,0:T(8,128)(2,1)} %copy-done.6) | copy-start | bytes 1572868
  97.0 22.3 %copy-start.9 = (bf16[128,2048]{1,0:T(8,128)(2,1)S(1)}, bf16[128,2048]{1,0:T(8,128)(2,1)}, u32[]{:S(2)}) copy-start(bf16[128,2048]{1,0:T(8,128)(2,1)} %copy-done.8) | copy-start | bytes 1572868
  97.0 2.7 %collective-permute-start.12 = (bf16[128,2048]{1,0:T(8,128)(2,1)}, bf16[128,2048]{1,0:T(8,128)(2,1)S(1)}, u32[]{:S(2)}, u32[]{:S(2)}) collective-permute-start(bf16[128,2048]{1,0:T(8,128)(2,1)} %copy-done.14), channel_id=1, source_target_pairs={{1,0},{0,1},{3,2},{2,3},{5,4},{4,5},{7,6},{6,7},{9,8},{8,9},{11,10... | collective-permute-start | bytes 1572872 | tf_op jit(solution)/shard_map/ppermute | solution.py:197
  97.5 3.1 %collective-permute-start.13 = (bf16[128,2048]{1,0:T(8,128)(2,1)}, bf16[128,2048]{1,0:T(8,128)(2,1)S(1)}, u32[]{:S(2)}, u32[]{:S(2)}) collective-permute-start(bf16[128,2048]{1,0:T(8,128)(2,1)} %copy-done.10), channel_id=1, source_target_pairs={{1,0},{0,1},{3,2},{2,3},{5,4},{4,5},{7,6},{6,7},{9,8},{8,9},{11,10... | collective-permute-start | bytes 1572872 | tf_op jit(solution)/shard_map/ppermute | solution.py:197
  97.6 3.8 %collective-permute-start.11 = (bf16[128,2048]{1,0:T(8,128)(2,1)}, bf16[128,2048]{1,0:T(8,128)(2,1)S(1)}, u32[]{:S(2)}, u32[]{:S(2)}) collective-permute-start(bf16[128,2048]{1,0:T(8,128)(2,1)} %collective-permute-done.4.refs_7_), channel_id=1, source_target_pairs={{1,0},{0,1},{3,2},{2,3},{5,4},{4,5},{7,6},{6,7},{9,8},{8,9},{11,10... | collective-permute-start | bytes 1572872 | tf_op jit(solution)/shard_map/ppermute | solution.py:197
  98.0 19.1 %collective-permute-start.10 = (bf16[128,2048]{1,0:T(8,128)(2,1)}, bf16[128,2048]{1,0:T(8,128)(2,1)}, u32[]{:S(2)}, u32[]{:S(2)}) collective-permute-start(bf16[128,2048]{1,0:T(8,128)(2,1)} %collective-permute-done.4.refs_7_), channel_id=1, source_target_pairs={{2,0},{3,1},{0,2},{1,3},{6,4},{7,5},{4,6},{5,7},{10,8},{11,9},{8,1... | collective-permute-start | bytes 1572872 | tf_op jit(solution)/shard_map/ppermute | solution.py:197
  99.7 0.9 copy-start.16
  100.5 0.8 copy-start.18
  101.4 0.8 copy-start.20
  117.1 2.3 %collective-permute-start.14 = (bf16[128,2048]{1,0:T(8,128)(2,1)}, bf16[128,2048]{1,0:T(8,128)(2,1)}, u32[]{:S(2)}, u32[]{:S(2)}) collective-permute-start(bf16[128,2048]{1,0:T(8,128)(2,1)} %collective-permute-done.10.refs_13_), channel_id=1, source_target_pairs={{1,0},{0,1},{3,2},{2,3},{5,4},{4,5},{7,6},{6,7},{9,8},{8,9},{11,10... | collective-permute-start | bytes 1572872 | tf_op jit(solution)/shard_map/ppermute | solution.py:197
  119.3 1.0 copy-start.11
  120.4 1.0 copy-start.13
  121.4 1.0 copy-start.15
  122.5 1.0 copy-start.17
  123.5 1.0 copy-start.19
  124.6 1.0 copy-start.21

commit v3 on v0

v3 whole, which is shorter than its diff:
```python
import functools

import jax
import jax.numpy as jnp
import numpy as np
from jax import lax
from jax.experimental import pallas as pl
from jax.experimental.pallas import tpu as pltpu
from jax.sharding import PartitionSpec as P

TS = 32
VT = 4
NTP = VT * VT
LANES = 128
GROUPS = LANES // TS
STRIPES = TS // GROUPS
SIDES = 2
CORES = 2
MIB = 1024 * 1024

VMEM = pl.BlockSpec(memory_space=pltpu.VMEM)
SMEM = pl.BlockSpec(memory_space=pltpu.SMEM)


def swap_groups(four):
    lane = lax.broadcasted_iota(jnp.int32, four[0].shape, four[0].ndim - 1)
    low = lane < 2 * TS
    even = (lane // TS) % 2 == 0
    v = list(four)
    for p in (0, 1):
        a, b = v[p], v[p + 2]
        v[p] = jnp.where(low, a, pltpu.roll(b, 2 * TS, 1))
        v[p + 2] = jnp.where(low, pltpu.roll(a, 2 * TS, 1), b)
    for p in (0, 2):
        a, b = v[p], v[p + 1]
        v[p] = jnp.where(even, a, pltpu.roll(b, TS, 1))
        v[p + 1] = jnp.where(even, pltpu.roll(a, LANES - TS, 1), b)
    return v


def stripe(h):
    return slice(h * LANES, (h + 1) * LANES)


def ladder_kernel(arrived_ref, ints_ref, amps_ref, out_ref, total):
    occ = out_ref.shape[0]
    out_ref[:, occ:, :] = amps_ref[0]
    value = jnp.dot(
        arrived_ref[...].reshape(occ * occ, TS * TS),
        ints_ref[0],
        preferred_element_type=jnp.float32,
    )
    for h in range(STRIPES):
        total[h] = value[:, stripe(h)]
        for j in range(occ):
            rows = total[h, pl.ds(j, occ, stride=occ), :]
            out_ref[j, :occ, stripe(h)] = rows.astype(jnp.bfloat16)


def ladder_partial(arrived, ladder_ints, amps):
    occ = arrived.shape[0]
    return pl.pallas_call(
        ladder_kernel,
        out_shape=jax.ShapeDtypeStruct((occ, occ + NTP, TS * TS), jnp.bfloat16),
        in_specs=[VMEM] * 3,
        out_specs=VMEM,
        scratch_shapes=[pltpu.VMEM((STRIPES, occ * occ, LANES), jnp.float32)],
        compiler_params=pltpu.CompilerParams(vmem_limit_bytes=24 * MIB),
        cost_estimate=pl.CostEstimate(
            flops=2 * occ * occ * TS**4, bytes_accessed=2 * TS**4, transcendentals=0
        ),
    )(arrived, ladder_ints, amps)


def finish_kernel(me, table, targets, moved_ref, *rest):
    count = len(rest) - 5
    pieces = rest[:count]
    out_ref, ladder, columns, product, result = rest[count:]
    occ = out_ref.shape[0]
    if occ == NTP:
        for q in range(occ):
            ladder[targets[q]] = moved_ref[q, :occ].astype(jnp.float32)
    else:
        ladder[...] = jnp.zeros_like(ladder)
        for q in range(occ):
            ladder[targets[q]] += moved_ref[q, :occ].astype(jnp.float32)
    for h in range(STRIPES):
        wide = moved_ref[:, occ:, stripe(h)].astype(jnp.float32)
        result[h] = wide.reshape(occ * NTP, LANES)
    for C in range(VT):
        for h in range(STRIPES):
            four = []
            for B in range(VT):
                pair = C * VT + B
                amp = result[h, pl.ds(pair, occ, stride=NTP), :]
                four.append(amp + ladder[pair, :, stripe(h)])
            for g, value in enumerate(swap_groups(four)):
                columns[pl.ds(C * TS + h * GROUPS + g, occ, stride=VT * TS), :] = value
    right = columns[...].astype(jnp.bfloat16)

    for n, piece in enumerate(pieces):
        rows = piece.shape[0]
        start = pl.multiple_of(table[me[0], n] * rows, rows)
        product[pl.ds(start, rows), :] = jnp.dot(
            piece[...], right, preferred_element_type=jnp.float32
        )

    for h in range(STRIPES):
        for A in range(VT):
            four = [
                product[pl.ds(A * TS + h * GROUPS + g, occ, stride=VT * TS), :]
                for g in range(GROUPS)
            ]
            for B, value in enumerate(swap_groups(four)):
                pair = A * VT + B
                total = value + ladder[pair, :, stripe(h)]
                result[h, pl.ds(pair, occ, stride=NTP), :] = total
        out_ref[:, :, stripe(h)] = result[h].astype(jnp.bfloat16).reshape(occ, NTP, LANES)


def finish(me, table, targets, moved, pieces):
    occ = moved.shape[0]
    rows = occ * VT * TS
    return pl.pallas_call(
        finish_kernel,
        out_shape=jax.ShapeDtypeStruct((occ, NTP, TS * TS), jnp.bfloat16),
        in_specs=[SMEM] * 3 + [VMEM] * (1 + len(pieces)),
        out_specs=VMEM,
        scratch_shapes=[
            pltpu.VMEM((NTP, occ, TS * TS), jnp.float32),
            pltpu.VMEM((rows, LANES), jnp.float32),
            pltpu.VMEM((rows, LANES), jnp.float32),
            pltpu.VMEM((STRIPES, occ * NTP, LANES), jnp.float32),
        ],
        compiler_params=pltpu.CompilerParams(vmem_limit_bytes=52 * MIB),
        cost_estimate=pl.CostEstimate(
            flops=2 * rows * rows * LANES, bytes_accessed=2 * rows * rows, transcendentals=0
        ),
    )(me, table, targets, moved, *pieces)


class Rows:
    def __init__(self, array, owners):
        self.array, self.owners = array, owners

    def moved(self, targets):
        perm = sorted(targets.items())
        owners = [0] * len(self.owners)
        for source, target in perm:
            owners[target] = self.owners[source]
        return Rows(lax.ppermute(self.array, "tile", perm), owners)


def choose(mask, yes, no):
    mine = jnp.asarray(np.array(mask, np.int32))[lax.axis_index("tile")] == 1
    owners = [y if m else n for m, y, n in zip(mask, yes.owners, no.owners)]
    return Rows(jnp.where(mine, yes.array, no.array), owners)


def member(line, side, core):
    return (line * SIDES + side) * CORES + core


def split(t):
    return t // (SIDES * CORES), t // CORES % SIDES, t % CORES


def along_line(own, members):
    line = [split(t)[0] for t in range(members)]

    def hop(*pairs):
        ends = dict(pairs)
        return {t: member(ends[line[t]], *split(t)[1:]) for t in range(members) if line[t] in ends}

    inner = hop((1, 2), (2, 1))
    outward = hop((1, 0), (2, 3))
    outer = [n in (0, 3) for n in line]
    first = own.moved(hop((0, 1), (1, 0), (2, 3), (3, 2)))
    third_in = own.moved(inner)
    second_in = first.moved(inner)
    second_out = third_in.moved(outward)
    third_out = second_in.moved(outward)
    near = [own, first, choose(outer, second_out, second_in), choose(outer, third_out, third_in)]
    return near, [second_in]


def along_ring(own, members):
    lines = members // (SIDES * CORES)
    ring = list(range(0, lines, 2)) + list(range(1, lines, 2))[::-1]
    place = {n: p for p, n in enumerate(ring)}

    def turn(step):
        targets = {}
        for t in range(members):
            line, side, core = split(t)
            ahead = step if core == 0 else -step
            targets[t] = member(ring[(place[line] + ahead) % lines], side, core)
        return targets

    blocks = [own]
    for step, count in ((1, lines // 2), (-1, (lines - 1) // 2)):
        last = own
        for _ in range(count):
            last = last.moved(turn(step))
            blocks.append(last)
    return blocks, []


def wait_for(value, blocks):
    return lax.optimization_barrier((value, [block.array for block in blocks]))[0]


def per_device(amps, ladder_ints, quad_pairs, cycle_ints):
    members = lax.axis_size("tile")
    swap = functools.partial(
        lax.all_to_all, axis_name="tile", split_axis=0, concat_axis=0, tiled=True
    )

    own = Rows(cycle_ints, list(range(members)))
    lines = members // (SIDES * CORES)
    near, soon = (along_line if lines == 4 else along_ring)(own, members)
    side = {t: member(split(t)[0], (split(t)[1] + 1) % SIDES, split(t)[2]) for t in range(members)}
    core = {t: member(*split(t)[:2], (split(t)[2] + 1) % CORES) for t in range(members)}
    over = [block.moved(side) for block in near]
    blocks = near + over
    blocks += [block.moved(core) for block in blocks]
    table = np.array([block.owners for block in blocks], np.int32).T
    me = lax.axis_index("tile").astype(jnp.int32)[None]

    pairs = swap(jnp.broadcast_to(quad_pairs, (members, 2)))
    targets, inputs = pairs[:, 0], pairs[:, 1]
    tiles = amps[0].transpose(1, 0, 2)
    wanted = wait_for(jnp.take(tiles, inputs, axis=0, mode="clip"), over[:1])
    arrived = swap(wanted)
    sent = wait_for(ladder_partial(arrived, ladder_ints, amps), over[1:2] + soon)
    moved = swap(sent)
    residual = finish(me, table, targets, moved, [block.array for block in blocks])
    return residual[:, None]


def solution(mesh):
    return jax.shard_map(
        per_device,
        mesh=mesh,
        in_specs=(
            P(("frag", "tile"), None, None, None),
            P(("frag", "tile"), None, None),
            P(("frag", "tile"), None),
            P(("frag", "tile"), None),
        ),
        out_specs=P("frag", "tile", None, None),
        check_vma=False,
    )
```

time: 157 us -> 107 us (0.68)
  local copies, waits for them, and re-layouts: 36.2 us -> 7.66 us
  blocking collectives: 23.3 us -> 0 us
  starting transfers between devices: 26.5 us -> 39.6 us
  between operations: 13.5 us -> 0.78 us
  Pallas kernels: 0 us -> 11.1 us
  matrix products: 10.9 us -> 0 us
  waiting for transfers between devices: 34.4 us -> 45.1 us
  other arithmetic: 10.8 us -> 2.27 us
    ppermute x0 -> x17, waiting for transfers between devices: none -> 44.3 us  [moved(): return Rows(lax.ppermute(self.array, 'tile', perm), owners)]
    all_to_all x3, waiting for transfers between devices: 33.7 us -> 0.81 us  [the longest x1 0.8 us: per_device(): arrived = swap(wanted)]
    reshape x8 -> x0, local copies, waits for them, and re-layouts: 27.6 us -> none  [the longest x2 9.15 us: per_device(): cycle.reshape(all_occ, VT, TS, local_occ, VT, TS)]
    all_gather x1 -> x0, blocking collectives: 23.3 us -> none  [per_device(): all_quads = lax.all_gather(quad_pairs, 'tile', axis=0, tiled=True)]
    ppermute x0 -> x17, starting transfers between devices: none -> 16.5 us  [moved(): return Rows(lax.ppermute(self.array, 'tile', perm), owners)]
    pallas_call x0 -> x2, Pallas kernels: none -> 11.1 us  [the longest x1 9.02 us: finish(): pl.pallas_call(finish_kernel, out_shape=jax.ShapeDtypeStruct((occ, NTP, T...]
    dot_general x3 -> x0, matrix products: 10.9 us -> none  [the longest x1 6.49 us: per_device(): jnp.dot(lax.all_gather(cycle_ints, 'tile', axis=0, tiled=True), cycle_inp...]
    convert_element_type x2 -> x0, other arithmetic: 5.23 us -> none  [the longest x1 3.08 us: per_device(): updated = (amp_cycle.astype(jnp.float32) + ladder).astype(jnp.bfloat16)]
  transfers between devices with their start and end apart: 4 -> 20, of which waited for: 3 -> 6; matrix products, arithmetic and copies ran while one was open for 23% -> 6% of each run, Pallas kernels for 0% -> 2%
where the time goes in v3:
time: 107 us; the launch traced here: 106 us
  waiting for transfers between devices  45.1 us (42%)
  starting transfers between devices  39.6 us (37%)
  Pallas kernels  11.1 us (10%)
  local copies, waits for them, and re-layouts  7.66 us (7%)
  other arithmetic  2.27 us (2%)
    ppermute x17, waiting for transfers between devices, moved(): return Rows(lax.ppermute(self.array, 'tile', perm), owners)  44.3 us
    ppermute x17, starting transfers between devices, moved(): return Rows(lax.ppermute(self.array, 'tile', perm), owners)  16.5 us
    all_to_all x1, starting transfers between devices, per_device(): moved = swap(sent)  12.6 us
    pallas_call x1, Pallas kernels, finish(): pl.pallas_call(finish_kernel, out_shape=jax.ShapeDtypeStruct((occ, NTP, T...  9.02 us
    all_to_all x1, starting transfers between devices, per_device(): arrived = swap(wanted)  5.35 us
    all_to_all x1, starting transfers between devices, per_device(): pairs = swap(jnp.broadcast_to(quad_pairs, (members, 2)))  5.15 us
    unnamed x29, local copies, waits for them, and re-layouts  4.39 us
    select_n x2, other arithmetic, choose(): return Rows(jnp.where(mine, yes.array, no.array), owners)  2.26 us
  transfers between devices with their start and end apart: 20, of which 6 were waited for; matrix products, arithmetic and copies ran while one was open for 6% of the time, Pallas kernels for 2%

profile of v3, /device:TPU:0, one launch (start us, length us, event | category | flops | bytes accessed | tf_op | source)
XLA Modules:
  0.0 106.5 jit_solution(9538977468579113043)
XLA Ops:
  0.0 3.0 %collective-permute-start = (bf16[128,2048]{1,0:T(8,128)(2,1)}, bf16[128,2048]{1,0:T(8,128)(2,1)}, u32[]{:S(2)}, u32[]{:S(2)}) collective-permute-start(bf16[128,2048]{1,0:T(8,128)(2,1)} %rest_0_.1), channel_id=1, source_target_pairs={{0,2},{1,3},{2,0},{3,1},{4,6},{5,7},{6,4},{7,5},{8,10},{9,11},{10,... | collective-permute-start | bytes 1572872 | tf_op jit(solution)/shard_map/ppermute | solution.py:151
  3.0 1.3 %broadcast_in_dim.14 = s32[16,1,2]{2,1,0:T(1,128)} broadcast(s32[2]{0:T(128)} %bitcast.18), dimensions={2} | broadcast | bytes 136 | tf_op jit(solution)/shard_map/broadcast_in_dim | solution.py:230
  4.3 5.1 %all-to-all-start = ((s32[16,1,2]{2,1,0:T(1,128)}), s32[16,1,2]{2,1,0:T(1,128)S(1)}, u32[]{:S(2)}, u32[]{:S(2)}) async-start(s32[16,1,2]{2,1,0:T(1,128)} %broadcast_in_dim.14), calls=%async_computation | async-start | bytes 16384 | tf_op jit(solution)/shard_map/all_to_all | solution.py:230
  9.5 1.5 %collective-permute-start.4 = (bf16[128,2048]{1,0:T(8,128)(2,1)}, bf16[128,2048]{1,0:T(8,128)(2,1)}, u32[]{:S(2)}, u32[]{:S(2)}) collective-permute-start(bf16[128,2048]{1,0:T(8,128)(2,1)} %rest_0_.1), channel_id=1, source_target_pairs={{4,8},{5,9},{6,10},{7,11},{8,4},{9,5},{10,6},{11,7},{20,24},{21,25... | collective-permute-start | bytes 1572872 | tf_op jit(solution)/shard_map/ppermute | solution.py:151
  10.9 3.9 %collective-permute-start.1 = (bf16[128,2048]{1,0:T(8,128)(2,1)}, bf16[128,2048]{1,0:T(8,128)(2,1)}, u32[]{:S(2)}, u32[]{:S(2)}) collective-permute-start(bf16[128,2048]{1,0:T(8,128)(2,1)} %rest_0_.1), channel_id=1, source_target_pairs={{0,4},{1,5},{2,6},{3,7},{4,0},{5,1},{6,2},{7,3},{8,12},{9,13},{10,... | collective-permute-start | bytes 1572872 | tf_op jit(solution)/shard_map/ppermute | solution.py:151
  14.8 1.3 %copy.15 = bf16[1,16,16,1024]{3,1,2,0:T(8,128)(2,1)S(1)} copy(bf16[1,16,16,1024]{3,2,1,0:T(8,128)(2,1)} %amps_ref.1) | data formatting | bytes 1048576 | tf_op args[0]
  16.2 0.0 all-to-all-done
  16.2 0.1 copy.11
  16.3 1.4 %gather_fusion = bf16[16,16,1024]{2,1,0:T(8,128)(2,1)} fusion(bf16[16,16,1024]{2,1,0:T(8,128)(2,1)S(1)} %bitcast.16, s32[1024]{0:T(1024)S(1)} %pad_clamp_fusion), kind=kCustom, calls=%fused_computation | custom fusion | bytes 1048640 | tf_op jit(solution)/shard_map/jit(_take)/gather | solution.py:233
  17.6 0.0 collective-permute-done.rest_4_
  17.6 5.4 %all-to-all-start.1 = ((bf16[16,16,1024]{2,1,0:T(8,128)(2,1)}), bf16[16,16,1024]{2,1,0:T(8,128)(2,1)S(1)}, u32[]{:S(2)}, u32[]{:S(2)}) async-start(bf16[16,16,1024]{2,1,0:T(8,128)(2,1)} %gather_fusion), calls=%async_computation.1 | async-start | bytes 1048576 | tf_op jit(solution)/shard_map/all_to_all | solution.py:234
  23.0 7.3 %collective-permute-done.1.rest_1_ = bf16[128,2048]{1,0:T(8,128)(2,1)} collective-permute-done((bf16[128,2048]{1,0:T(8,128)(2,1)}, bf16[128,2048]{1,0:T(8,128)(2,1)}, u32[]{:S(2)}, u32[]{:S(2)}) %collective-permute-start.1) | collective-permute-done | bytes 524320 | tf_op jit(solution)/shard_map/ppermute | solution.py:151
  30.3 1.5 %collective-permute-start.3 = (bf16[128,2048]{1,0:T(8,128)(2,1)}, bf16[128,2048]{1,0:T(8,128)(2,1)}, u32[]{:S(2)}, u32[]{:S(2)}) collective-permute-start(bf16[128,2048]{1,0:T(8,128)(2,1)} %collective-permute-done.1.rest_1_), channel_id=1, source_target_pairs={{4,8},{5,9},{6,10},{7,11},{8,4},{9,5},{10,6},{11,7},{20,24},{21,25... | collective-permute-start | bytes 1572872 | tf_op jit(solution)/shard_map/ppermute | solution.py:151
  31.8 0.8 collective-permute-start.2
  32.5 0.0 collective-permute-done.4
  32.5 1.3 %collective-permute-start.5 = (bf16[128,2048]{1,0:T(8,128)(2,1)}, bf16[128,2048]{1,0:T(8,128)(2,1)}, u32[]{:S(2)}, u32[]{:S(2)}) collective-permute-start(bf16[128,2048]{1,0:T(8,128)(2,1)} %collective-permute-done.4), channel_id=1, source_target_pairs={{4,0},{5,1},{6,2},{7,3},{8,12},{9,13},{10,14},{11,15},{20,16},{21,... | collective-permute-start | bytes 1572872 | tf_op jit(solution)/shard_map/ppermute | solution.py:151
  33.8 0.1 collective-permute-start.9
  33.9 0.6 dynamic_slice.6
  35.0 0.5 collective-permute-start.10
  35.6 0.0 collective-permute-done.3
  35.6 1.3 %collective-permute-start.6 = (bf16[128,2048]{1,0:T(8,128)(2,1)}, bf16[128,2048]{1,0:T(8,128)(2,1)}, u32[]{:S(2)}, u32[]{:S(2)}) collective-permute-start(bf16[128,2048]{1,0:T(8,128)(2,1)} %collective-permute-done.3), channel_id=1, source_target_pairs={{4,0},{5,1},{6,2},{7,3},{8,12},{9,13},{10,14},{11,15},{20,16},{21,... | collective-permute-start | bytes 1572872 | tf_op jit(solution)/shard_map/ppermute | solution.py:151
  36.9 0.8 all-to-all-done.1.arrived_ref
  37.7 2.0 %shard_map.76 = bf16[16,32,1024]{2,1,0:T(8,128)(2,1)} custom-call(bf16[16,16,1024]{2,1,0:T(8,128)(2,1)S(1)} %all-to-all-done.1.arrived_ref, bf16[1,1024,1024]{2,1,0:T(8,128)(2,1)S(1)} %copy-done, bf16[1,16,16,1024]{3,2,1,0:T(8,128)(2,1)S(1)} %copy-done.1), custom_call_target="tpu_custom_call" | custom-call | flops 536870912 | bytes 2097152 | tf_op jit(solution)/shard_map/pallas_call | solution.py:62
  39.7 5.1 %collective-permute-done.2.rest_5_ = bf16[128,2048]{1,0:T(8,128)(2,1)} collective-permute-done((bf16[128,2048]{1,0:T(8,128)(2,1)}, bf16[128,2048]{1,0:T(8,128)(2,1)}, u32[]{:S(2)}, u32[]{:S(2)}) %collective-permute-start.2) | collective-permute-done | bytes 524320 | tf_op jit(solution)/shard_map/ppermute | solution.py:151
  44.9 12.6 %all-to-all-start.2 = ((bf16[16,32,1024]{2,1,0:T(8,128)(2,1)}), bf16[16,32,1024]{2,1,0:T(8,128)(2,1)S(1)}, u32[]{:S(2)}, u32[]{:S(2)}) async-start(bf16[16,32,1024]{2,1,0:T(8,128)(2,1)} %shard_map.76), calls=%async_computation.2 | async-start | bytes 2097152 | tf_op jit(solution)/shard_map/all_to_all | solution.py:236
  57.5 0.0 copy-start.2
  57.5 0.0 copy-start.3
  57.5 0.0 collective-permute-done.5
  57.5 1.2 %broadcast_select_fusion.1.rest_2_ = bf16[128,2048]{1,0:T(8,128)(2,1)S(1)} fusion(bf16[128,2048]{1,0:T(8,128)(2,1)} %collective-permute-done.5, bf16[128,2048]{1,0:T(8,128)(2,1)} %collective-permute-done.3, pred[]{:T(512)} %bitcast.7), kind=kLoop, calls=%fused_computation.3 | loop fusion | flops 262144 | bytes 1572865 | tf_op jit(solution)/shard_map/jit(_where)/select_n | solution.py:157
  58.7 2.0 %collective-permute-start.7 = (bf16[128,2048]{1,0:T(8,128)(2,1)S(1)}, bf16[128,2048]{1,0:T(8,128)(2,1)S(1)}, u32[]{:S(2)}, u32[]{:S(2)}) collective-permute-start(bf16[128,2048]{1,0:T(8,128)(2,1)S(1)} %broadcast_select_fusion.1.rest_2_), channel_id=1, source_target_pairs={{0,2},{1,3},{2,0},{3,1},{4,6},{5,7},{6,4},{7,5},{8,10},{9,11},{10,... | collective-permute-start | bytes 1572872 | tf_op jit(solution)/shard_map/ppermute | solution.py:151
  60.6 8.1 %collective-permute-done.6 = bf16[128,2048]{1,0:T(8,128)(2,1)} collective-permute-done((bf16[128,2048]{1,0:T(8,128)(2,1)}, bf16[128,2048]{1,0:T(8,128)(2,1)}, u32[]{:S(2)}, u32[]{:S(2)}) %collective-permute-start.6) | collective-permute-done | bytes 524320 | tf_op jit(solution)/shard_map/ppermute | solution.py:151
  68.8 1.1 %broadcast_select_fusion.rest_3_ = bf16[128,2048]{1,0:T(8,128)(2,1)S(1)} fusion(bf16[128,2048]{1,0:T(8,128)(2,1)} %collective-permute-done.6, bf16[128,2048]{1,0:T(8,128)(2,1)} %collective-permute-done.4, pred[]{:T(512)} %bitcast.7), kind=kLoop, calls=%fused_computation.2 | loop fusion | flops 262144 | bytes 1572865 | tf_op jit(solution)/shard_map/jit(_where)/select_n | solution.py:157
  69.9 0.1 collective-permute-start.8
  70.0 0.0 collective-permute-start.11
  70.1 0.5 collective-permute-start.14
  70.6 0.0 collective-permute-done.13.rest_12_
  70.6 0.1 collective-permute-start.12
  70.7 12.9 %collective-permute-done.7.rest_6_ = bf16[128,2048]{1,0:T(8,128)(2,1)S(1)} collective-permute-done((bf16[128,2048]{1,0:T(8,128)(2,1)S(1)}, bf16[128,2048]{1,0:T(8,128)(2,1)S(1)}, u32[]{:S(2)}, u32[]{:S(2)}) %collective-permute-start.7) | collective-permute-done | bytes 524320 | tf_op jit(solution)/shard_map/ppermute | solution.py:151
  83.5 0.0 collective-permute-start.15
  83.5 10.8 %collective-permute-done.8.rest_7_ = bf16[128,2048]{1,0:T(8,128)(2,1)S(1)} collective-permute-done((bf16[128,2048]{1,0:T(8,128)(2,1)S(1)}, bf16[128,2048]{1,0:T(8,128)(2,1)S(1)}, u32[]{:S(2)}, u32[]{:S(2)}) %collective-permute-start.8) | collective-permute-done | bytes 524320 | tf_op jit(solution)/shard_map/ppermute | solution.py:151
  94.3 0.0 collective-permute-start.16
  94.4 0.7 copy-done.8
  95.1 0.2 copy-done.9
  95.3 0.1 copy-done.10
  95.4 0.2 copy-done.12
  95.6 0.8 copy-done.11
  96.5 0.9 copy-done.4
  97.4 9.0 %shard_map.77 = bf16[16,16,1024]{2,1,0:T(8,128)(2,1)} custom-call(s32[1]{0:T(128)} %bitcast.me, s32[16,16]{1,0:T(8,128)S(1)} %copy-done.3, s32[16]{0:T(128)S(1)} %get-tuple-element.10.targets, bf16[16,32,1024]{2,1,0:T(8,128)(2,1)} %copy-done.4, bf16[128,2048]{1,0:T(8,128)(2,1)S(1)} %copy-done.2, bf16[128,2048]{1,0:T(8,128)(2,1)} %collective-permute-done.1.rest_1_, ...), custom_call_target="tpu_custom_call" | custom-call | flops 1073741824 | bytes 8388608 | tf_op jit(solution)/shard_map/pallas_call | solution.py:124
  (31 shorter events, 0.1 us)
Async XLA Ops:
  0.0 33.9 %copy-start.13 = (s32[16]{0:T(128)S(1)}, s32[16]{0:T(128)}, u32[]{:S(2)}) copy-start(s32[16]{0:T(128)} %constant.16.clone) | copy-start | bytes 196
  0.0 37.7 %copy-start.1 = (bf16[1,16,16,1024]{3,2,1,0:T(8,128)(2,1)S(1)}, bf16[1,16,16,1024]{3,2,1,0:T(8,128)(2,1)}, u32[]{:S(2)}) copy-start(bf16[1,16,16,1024]{3,2,1,0:T(8,128)(2,1)} %amps_ref.1) | copy-start | bytes 1572868
  0.0 37.7 %copy-start = (bf16[1,1024,1024]{2,1,0:T(8,128)(2,1)S(1)}, bf16[1,1024,1024]{2,1,0:T(8,128)(2,1)}, u32[]{:S(2)}) copy-start(bf16[1,1024,1024]{2,1,0:T(8,128)(2,1)} %ints_ref.1) | copy-start | bytes 6291460
  0.0 17.6 %collective-permute-start = (bf16[128,2048]{1,0:T(8,128)(2,1)}, bf16[128,2048]{1,0:T(8,128)(2,1)}, u32[]{:S(2)}, u32[]{:S(2)}) collective-permute-start(bf16[128,2048]{1,0:T(8,128)(2,1)} %rest_0_.1), channel_id=1, source_target_pairs={{0,2},{1,3},{2,0},{3,1},{4,6},{5,7},{6,4},{7,5},{8,10},{9,11},{10,... | collective-permute-start | bytes 1572872 | tf_op jit(solution)/shard_map/ppermute | solution.py:151
  4.3 11.9 %all-to-all-start = ((s32[16,1,2]{2,1,0:T(1,128)}), s32[16,1,2]{2,1,0:T(1,128)S(1)}, u32[]{:S(2)}, u32[]{:S(2)}) async-start(s32[16,1,2]{2,1,0:T(1,128)} %broadcast_in_dim.14), calls=%async_computation | async-start | bytes 16384 | tf_op jit(solution)/shard_map/all_to_all | solution.py:230
  9.5 23.1 %collective-permute-start.4 = (bf16[128,2048]{1,0:T(8,128)(2,1)}, bf16[128,2048]{1,0:T(8,128)(2,1)}, u32[]{:S(2)}, u32[]{:S(2)}) collective-permute-start(bf16[128,2048]{1,0:T(8,128)(2,1)} %rest_0_.1), channel_id=1, source_target_pairs={{4,8},{5,9},{6,10},{7,11},{8,4},{9,5},{10,6},{11,7},{20,24},{21,25... | collective-permute-start | bytes 1572872 | tf_op jit(solution)/shard_map/ppermute | solution.py:151
  10.9 19.4 %collective-permute-start.1 = (bf16[128,2048]{1,0:T(8,128)(2,1)}, bf16[128,2048]{1,0:T(8,128)(2,1)}, u32[]{:S(2)}, u32[]{:S(2)}) collective-permute-start(bf16[128,2048]{1,0:T(8,128)(2,1)} %rest_0_.1), channel_id=1, source_target_pairs={{0,4},{1,5},{2,6},{3,7},{4,0},{5,1},{6,2},{7,3},{8,12},{9,13},{10,... | collective-permute-start | bytes 1572872 | tf_op jit(solution)/shard_map/ppermute | solution.py:151
  17.6 20.0 %all-to-all-start.1 = ((bf16[16,16,1024]{2,1,0:T(8,128)(2,1)}), bf16[16,16,1024]{2,1,0:T(8,128)(2,1)S(1)}, u32[]{:S(2)}, u32[]{:S(2)}) async-start(bf16[16,16,1024]{2,1,0:T(8,128)(2,1)} %gather_fusion), calls=%async_computation.1 | async-start | bytes 1048576 | tf_op jit(solution)/shard_map/all_to_all | solution.py:234
  30.3 5.3 %collective-permute-start.3 = (bf16[128,2048]{1,0:T(8,128)(2,1)}, bf16[128,2048]{1,0:T(8,128)(2,1)}, u32[]{:S(2)}, u32[]{:S(2)}) collective-permute-start(bf16[128,2048]{1,0:T(8,128)(2,1)} %collective-permute-done.1.rest_1_), channel_id=1, source_target_pairs={{4,8},{5,9},{6,10},{7,11},{8,4},{9,5},{10,6},{11,7},{20,24},{21,25... | collective-permute-start | bytes 1572872 | tf_op jit(solution)/shard_map/ppermute | solution.py:151
  31.8 13.1 %collective-permute-start.2 = (bf16[128,2048]{1,0:T(8,128)(2,1)}, bf16[128,2048]{1,0:T(8,128)(2,1)}, u32[]{:S(2)}, u32[]{:S(2)}) collective-permute-start(bf16[128,2048]{1,0:T(8,128)(2,1)} %collective-permute-done.1.rest_1_), channel_id=1, source_target_pairs={{0,2},{1,3},{2,0},{3,1},{4,6},{5,7},{6,4},{7,5},{8,10},{9,11},{10,... | collective-permute-start | bytes 1572872 | tf_op jit(solution)/shard_map/ppermute | solution.py:151
  32.5 24.9 %collective-permute-start.5 = (bf16[128,2048]{1,0:T(8,128)(2,1)}, bf16[128,2048]{1,0:T(8,128)(2,1)}, u32[]{:S(2)}, u32[]{:S(2)}) collective-permute-start(bf16[128,2048]{1,0:T(8,128)(2,1)} %collective-permute-done.4), channel_id=1, source_target_pairs={{4,0},{5,1},{6,2},{7,3},{8,12},{9,13},{10,14},{11,15},{20,16},{21,... | collective-permute-start | bytes 1572872 | tf_op jit(solution)/shard_map/ppermute | solution.py:151
  33.8 36.2 %collective-permute-start.9 = (bf16[128,2048]{1,0:T(8,128)(2,1)}, bf16[128,2048]{1,0:T(8,128)(2,1)}, u32[]{:S(2)}, u32[]{:S(2)}) collective-permute-start(bf16[128,2048]{1,0:T(8,128)(2,1)} %rest_0_.1), channel_id=1, source_target_pairs={{0,1},{1,0},{2,3},{3,2},{4,5},{5,4},{6,7},{7,6},{8,9},{9,8},{10,11... | collective-permute-start | bytes 1572872 | tf_op jit(solution)/shard_map/ppermute | solution.py:151
  35.0 35.0 %collective-permute-start.10 = (bf16[128,2048]{1,0:T(8,128)(2,1)}, bf16[128,2048]{1,0:T(8,128)(2,1)}, u32[]{:S(2)}, u32[]{:S(2)}) collective-permute-start(bf16[128,2048]{1,0:T(8,128)(2,1)} %collective-permute-done.1.rest_1_), channel_id=1, source_target_pairs={{0,1},{1,0},{2,3},{3,2},{4,5},{5,4},{6,7},{7,6},{8,9},{9,8},{10,11... | collective-permute-start | bytes 1572872 | tf_op jit(solution)/shard_map/ppermute | solution.py:151
  35.6 33.2 %collective-permute-start.6 = (bf16[128,2048]{1,0:T(8,128)(2,1)}, bf16[128,2048]{1,0:T(8,128)(2,1)}, u32[]{:S(2)}, u32[]{:S(2)}) collective-permute-start(bf16[128,2048]{1,0:T(8,128)(2,1)} %collective-permute-done.3), channel_id=1, source_target_pairs={{4,0},{5,1},{6,2},{7,3},{8,12},{9,13},{10,14},{11,15},{20,16},{21,... | collective-permute-start | bytes 1572872 | tf_op jit(solution)/shard_map/ppermute | solution.py:151
  44.8 25.7 %collective-permute-start.13 = (bf16[128,2048]{1,0:T(8,128)(2,1)}, bf16[128,2048]{1,0:T(8,128)(2,1)S(1)}, u32[]{:S(2)}, u32[]{:S(2)}) collective-permute-start(bf16[128,2048]{1,0:T(8,128)(2,1)} %collective-permute-done.rest_4_), channel_id=1, source_target_pairs={{0,1},{1,0},{2,3},{3,2},{4,5},{5,4},{6,7},{7,6},{8,9},{9,8},{10,11... | collective-permute-start | bytes 1572872 | tf_op jit(solution)/shard_map/ppermute | solution.py:151
  44.9 51.6 %all-to-all-start.2 = ((bf16[16,32,1024]{2,1,0:T(8,128)(2,1)}), bf16[16,32,1024]{2,1,0:T(8,128)(2,1)S(1)}, u32[]{:S(2)}, u32[]{:S(2)}) async-start(bf16[16,32,1024]{2,1,0:T(8,128)(2,1)} %shard_map.76), calls=%async_computation.2 | async-start | bytes 2097152 | tf_op jit(solution)/shard_map/all_to_all | solution.py:236
  57.5 40.0 %copy-start.2 = (bf16[128,2048]{1,0:T(8,128)(2,1)S(1)}, bf16[128,2048]{1,0:T(8,128)(2,1)}, u32[]{:S(2)}) copy-start(bf16[128,2048]{1,0:T(8,128)(2,1)} %rest_0_.1) | copy-start | bytes 1572868
  57.5 40.0 %copy-start.3 = (s32[16,16]{1,0:T(8,128)S(1)}, s32[16,16]{1,0:T(8,128)}, u32[]{:S(2)}) copy-start(s32[16,16]{1,0:T(8,128)} %constant.17.clone.table) | copy-start | bytes 3076
  58.7 24.9 %collective-permute-start.7 = (bf16[128,2048]{1,0:T(8,128)(2,1)S(1)}, bf16[128,2048]{1,0:T(8,128)(2,1)S(1)}, u32[]{:S(2)}, u32[]{:S(2)}) collective-permute-start(bf16[128,2048]{1,0:T(8,128)(2,1)S(1)} %broadcast_select_fusion.1.rest_2_), channel_id=1, source_target_pairs={{0,2},{1,3},{2,0},{3,1},{4,6},{5,7},{6,4},{7,5},{8,10},{9,11},{10,... | collective-permute-start | bytes 1572872 | tf_op jit(solution)/shard_map/ppermute | solution.py:151
  69.9 26.6 %copy-start.5 = (bf16[128,2048]{1,0:T(8,128)(2,1)}, bf16[128,2048]{1,0:T(8,128)(2,1)S(1)}, u32[]{:S(2)}) copy-start(bf16[128,2048]{1,0:T(8,128)(2,1)S(1)} %broadcast_select_fusion.rest_3_) | copy-start | bytes 1572868
  69.9 24.4 %collective-permute-start.8 = (bf16[128,2048]{1,0:T(8,128)(2,1)S(1)}, bf16[128,2048]{1,0:T(8,128)(2,1)S(1)}, u32[]{:S(2)}, u32[]{:S(2)}) collective-permute-start(bf16[128,2048]{1,0:T(8,128)(2,1)S(1)} %broadcast_select_fusion.rest_3_), channel_id=1, source_target_pairs={{0,2},{1,3},{2,0},{3,1},{4,6},{5,7},{6,4},{7,5},{8,10},{9,11},{10,... | collective-permute-start | bytes 1572872 | tf_op jit(solution)/shard_map/ppermute | solution.py:151
  70.0 24.3 %collective-permute-start.11 = (bf16[128,2048]{1,0:T(8,128)(2,1)S(1)}, bf16[128,2048]{1,0:T(8,128)(2,1)S(1)}, u32[]{:S(2)}, u32[]{:S(2)}) collective-permute-start(bf16[128,2048]{1,0:T(8,128)(2,1)S(1)} %broadcast_select_fusion.1.rest_2_), channel_id=1, source_target_pairs={{0,1},{1,0},{2,3},{3,2},{4,5},{5,4},{6,7},{7,6},{8,9},{9,8},{10,11... | collective-permute-start | bytes 1572872 | tf_op jit(solution)/shard_map/ppermute | solution.py:151
  70.1 24.2 %collective-permute-start.14 = (bf16[128,2048]{1,0:T(8,128)(2,1)}, bf16[128,2048]{1,0:T(8,128)(2,1)S(1)}, u32[]{:S(2)}, u32[]{:S(2)}) collective-permute-start(bf16[128,2048]{1,0:T(8,128)(2,1)} %collective-permute-done.2.rest_5_), channel_id=1, source_target_pairs={{0,1},{1,0},{2,3},{3,2},{4,5},{5,4},{6,7},{7,6},{8,9},{9,8},{10,11... | collective-permute-start | bytes 1572872 | tf_op jit(solution)/shard_map/ppermute | solution.py:151
  70.6 25.9 %copy-start.6 = (bf16[128,2048]{1,0:T(8,128)(2,1)}, bf16[128,2048]{1,0:T(8,128)(2,1)S(1)}, u32[]{:S(2)}) copy-start(bf16[128,2048]{1,0:T(8,128)(2,1)S(1)} %collective-permute-done.13.rest_12_) | copy-start | bytes 1572868
  70.6 23.8 %collective-permute-start.12 = (bf16[128,2048]{1,0:T(8,128)(2,1)S(1)}, bf16[128,2048]{1,0:T(8,128)(2,1)S(1)}, u32[]{:S(2)}, u32[]{:S(2)}) collective-permute-start(bf16[128,2048]{1,0:T(8,128)(2,1)S(1)} %broadcast_select_fusion.rest_3_), channel_id=1, source_target_pairs={{0,1},{1,0},{2,3},{3,2},{4,5},{5,4},{6,7},{7,6},{8,9},{9,8},{10,11... | collective-permute-start | bytes 1572872 | tf_op jit(solution)/shard_map/ppermute | solution.py:151
  83.5 10.8 %copy-start.7 = (bf16[128,2048]{1,0:T(8,128)(2,1)}, bf16[128,2048]{1,0:T(8,128)(2,1)S(1)}, u32[]{:S(2)}) copy-start(bf16[128,2048]{1,0:T(8,128)(2,1)S(1)} %collective-permute-done.7.rest_6_) | copy-start | bytes 1572868
  83.5 10.8 %collective-permute-start.15 = (bf16[128,2048]{1,0:T(8,128)(2,1)S(1)}, bf16[128,2048]{1,0:T(8,128)(2,1)S(1)}, u32[]{:S(2)}, u32[]{:S(2)}) collective-permute-start(bf16[128,2048]{1,0:T(8,128)(2,1)S(1)} %collective-permute-done.7.rest_6_), channel_id=1, source_target_pairs={{0,1},{1,0},{2,3},{3,2},{4,5},{5,4},{6,7},{7,6},{8,9},{9,8},{10,11... | collective-permute-start | bytes 1572872 | tf_op jit(solution)/shard_map/ppermute | solution.py:151
  94.3 0.8 copy-start.8
  94.3 2.2 %collective-permute-start.16 = (bf16[128,2048]{1,0:T(8,128)(2,1)S(1)}, bf16[128,2048]{1,0:T(8,128)(2,1)}, u32[]{:S(2)}, u32[]{:S(2)}) collective-permute-start(bf16[128,2048]{1,0:T(8,128)(2,1)S(1)} %collective-permute-done.8.rest_7_), channel_id=1, source_target_pairs={{0,1},{1,0},{2,3},{3,2},{4,5},{5,4},{6,7},{7,6},{8,9},{9,8},{10,11... | collective-permute-start | bytes 1572872 | tf_op jit(solution)/shard_map/ppermute | solution.py:151
  94.3 1.0 copy-start.9
  94.3 1.1 %copy-start.10 = (bf16[128,2048]{1,0:T(8,128)(2,1)}, bf16[128,2048]{1,0:T(8,128)(2,1)S(1)}, u32[]{:S(2)}) copy-start(bf16[128,2048]{1,0:T(8,128)(2,1)S(1)} %collective-permute-done.14.rest_13_) | copy-start | bytes 1572868
  94.3 1.3 %copy-start.12 = (bf16[128,2048]{1,0:T(8,128)(2,1)}, bf16[128,2048]{1,0:T(8,128)(2,1)S(1)}, u32[]{:S(2)}) copy-start(bf16[128,2048]{1,0:T(8,128)(2,1)S(1)} %collective-permute-done.15.rest_14_) | copy-start | bytes 1572868
  95.6 0.8 copy-start.11
  96.4 1.0 copy-start.4

commit v4 on v3

--- a/solution.py
+++ b/solution.py
@@ -11,6 +11,7 @@
 TS = 32
 VT = 4
 NTP = VT * VT
+AHEAD = NTP // 2
 LANES = 128
 GROUPS = LANES // TS
 STRIPES = TS // GROUPS
@@ -44,7 +45,7 @@
 
 def ladder_kernel(arrived_ref, ints_ref, amps_ref, out_ref, total):
     occ = out_ref.shape[0]
-    out_ref[:, occ:, :] = amps_ref[0]
+    out_ref[:, occ:, :] = amps_ref[0, :, AHEAD:, :]
     value = jnp.dot(
         arrived_ref[...].reshape(occ * occ, TS * TS),
         ints_ref[0],
@@ -61,7 +62,7 @@
     occ = arrived.shape[0]
     return pl.pallas_call(
         ladder_kernel,
-        out_shape=jax.ShapeDtypeStruct((occ, occ + NTP, TS * TS), jnp.bfloat16),
+        out_shape=jax.ShapeDtypeStruct((occ, occ + NTP - AHEAD, TS * TS), jnp.bfloat16),
         in_specs=[VMEM] * 3,
         out_specs=VMEM,
         scratch_shapes=[pltpu.VMEM((STRIPES, occ * occ, LANES), jnp.float32)],
@@ -72,7 +73,7 @@
     )(arrived, ladder_ints, amps)
 
 
-def finish_kernel(me, table, targets, moved_ref, *rest):
+def finish_kernel(me, table, targets, ahead_ref, moved_ref, *rest):
     count = len(rest) - 5
     pieces = rest[:count]
     out_ref, ladder, columns, product, result = rest[count:]
@@ -85,7 +86,8 @@
         for q in range(occ):
             ladder[targets[q]] += moved_ref[q, :occ].astype(jnp.float32)
     for h in range(STRIPES):
-        wide = moved_ref[:, occ:, stripe(h)].astype(jnp.float32)
+        halves = [ahead_ref[:, :, stripe(h)], moved_ref[:, occ:, stripe(h)]]
+        wide = jnp.concatenate([half.astype(jnp.float32) for half in halves], axis=1)
         result[h] = wide.reshape(occ * NTP, LANES)
     for C in range(VT):
         for h in range(STRIPES):
@@ -118,13 +120,13 @@
         out_ref[:, :, stripe(h)] = result[h].astype(jnp.bfloat16).reshape(occ, NTP, LANES)
 
 
-def finish(me, table, targets, moved, pieces):
+def finish(me, table, targets, ahead, moved, pieces):
     occ = moved.shape[0]
     rows = occ * VT * TS
     return pl.pallas_call(
         finish_kernel,
         out_shape=jax.ShapeDtypeStruct((occ, NTP, TS * TS), jnp.bfloat16),
-        in_specs=[SMEM] * 3 + [VMEM] * (1 + len(pieces)),
+        in_specs=[SMEM] * 3 + [VMEM] * (2 + len(pieces)),
         out_specs=VMEM,
         scratch_shapes=[
             pltpu.VMEM((NTP, occ, TS * TS), jnp.float32),
@@ -136,7 +138,7 @@
         cost_estimate=pl.CostEstimate(
             flops=2 * rows * rows * LANES, bytes_accessed=2 * rows * rows, transcendentals=0
         ),
-    )(me, table, targets, moved, *pieces)
+    )(me, table, targets, ahead, moved, *pieces)
 
 
 class Rows:
@@ -180,7 +182,7 @@
     second_in = first.moved(inner)
     second_out = third_in.moved(outward)
     third_out = second_in.moved(outward)
-    near = [own, first, choose(outer, second_out, second_in), choose(outer, third_out, third_in)]
+    near = [own, first, choose(outer, second_out, third_in), choose(outer, third_out, second_in)]
     return near, [second_in]
 
 
@@ -227,14 +229,17 @@
     table = np.array([block.owners for block in blocks], np.int32).T
     me = lax.axis_index("tile").astype(jnp.int32)[None]
 
-    pairs = swap(jnp.broadcast_to(quad_pairs, (members, 2)))
-    targets, inputs = pairs[:, 0], pairs[:, 1]
+    tags = jnp.repeat(quad_pairs.astype(jnp.bfloat16), LANES // 2, axis=1)[:, None, :]
+    tags = jnp.broadcast_to(tags, (members, AHEAD, LANES))
+    ahead = swap(jnp.concatenate([amps[0, :, :AHEAD], tags], axis=2))
+    pairs = ahead[:, 0, TS * TS:].astype(jnp.int32)
+    targets, inputs = pairs[:, 0], pairs[:, LANES // 2]
     tiles = amps[0].transpose(1, 0, 2)
     wanted = wait_for(jnp.take(tiles, inputs, axis=0, mode="clip"), over[:1])
     arrived = swap(wanted)
     sent = wait_for(ladder_partial(arrived, ladder_ints, amps), over[1:2] + soon)
     moved = swap(sent)
-    residual = finish(me, table, targets, moved, [block.array for block in blocks])
+    residual = finish(me, table, targets, ahead, moved, [block.array for block in blocks])
     return residual[:, None]
 
 

time: 107 us -> 107 us (level)
  waiting for transfers between devices: 45.1 us -> 39.7 us
  starting transfers between devices: 39.6 us -> 44.1 us
  other arithmetic: 2.27 us -> 3.66 us
    ppermute x17, waiting for transfers between devices: 44.3 us -> 30.4 us  [moved(): return Rows(lax.ppermute(self.array, 'tile', perm), owners)]
    all_to_all x1, waiting for transfers between devices: 0.8 us -> 9.34 us  [per_device(): arrived = swap(wanted)]
    all_to_all x1, starting transfers between devices: 12.6 us -> 5.29 us  [per_device(): moved = swap(sent)]
    ppermute x17, starting transfers between devices: 16.5 us -> 22.1 us  [moved(): return Rows(lax.ppermute(self.array, 'tile', perm), owners)]
    all_to_all x1, starting transfers between devices: 5.35 us -> 9.33 us  [per_device(): arrived = swap(wanted)]
    all_to_all x1, starting transfers between devices: 5.15 us -> 7.39 us  [per_device(): ahead = swap(jnp.concatenate([amps[0, :, :AHEAD], tags], axis=2))]
    broadcast_in_dim x1 -> x2, local copies, waits for them, and re-layouts: 1.26 us -> 0.16 us  [per_device(): jnp.repeat(quad_pairs.astype(jnp.bfloat16), LANES // 2, axis=1)[:, None, :]]
    unnamed x29 -> x25, local copies, waits for them, and re-layouts: 4.39 us -> 4.4 us
  transfers between devices with their start and end apart: 20 -> 20, of which waited for: 6 -> 7; matrix products, arithmetic and copies ran while one was open for 6% -> 5% of each run, Pallas kernels for 2% -> 2%
where the time goes in v4:
time: 107 us
  starting transfers between devices  44.1 us (41%)
  waiting for transfers between devices  39.7 us (37%)
  Pallas kernels  10.7 us (10%)
  local copies, waits for them, and re-layouts  7.69 us (7%)
  other arithmetic  3.66 us (3%)
    ppermute x17, waiting for transfers between devices, moved(): return Rows(lax.ppermute(self.array, 'tile', perm), owners)  30.4 us
    ppermute x17, starting transfers between devices, moved(): return Rows(lax.ppermute(self.array, 'tile', perm), owners)  22.1 us
    all_to_all x1, waiting for transfers between devices, per_device(): arrived = swap(wanted)  9.34 us
    all_to_all x1, starting transfers between devices, per_device(): arrived = swap(wanted)  9.33 us
    pallas_call x1, Pallas kernels, finish(): pl.pallas_call(finish_kernel, out_shape=jax.ShapeDtypeStruct((occ, NTP, T...  8.78 us
    all_to_all x1, starting transfers between devices, per_device(): ahead = swap(jnp.concatenate([amps[0, :, :AHEAD], tags], axis=2))  7.39 us
    all_to_all x1, starting transfers between devices, per_device(): moved = swap(sent)  5.29 us
    unnamed x25, local copies, waits for them, and re-layouts  4.4 us
  transfers between devices with their start and end apart: 20, of which 7 were waited for; matrix products, arithmetic and copies ran while one was open for 5% of the time, Pallas kernels for 2%

profile of v4, /device:TPU:0, one launch (start us, length us, event | category | flops | bytes accessed | tf_op | source)
XLA Modules:
  0.0 106.8 jit_solution(1966054742247215258)
XLA Ops:
  0.0 0.7 convert_bitcast_fusion
  0.7 0.1 broadcast_in_dim.19
  0.7 0.1 reshape.21
  0.8 1.0 slice_bitcast_fusion
  1.8 0.0 copy-start.2
  1.8 0.0 copy-start.11
  1.8 0.8 pad_maximum_fusion
  2.6 7.4 %all-to-all-start = ((bf16[16,8,1152]{2,1,0:T(8,128)(2,1)}), bf16[16,8,1152]{2,1,0:T(8,128)(2,1)S(1)}, u32[]{:S(2)}, u32[]{:S(2)}) async-start(bf16[16,8,1152]{2,1,0:T(8,128)(2,1)} %pad_maximum_fusion), calls=%async_computation | async-start | bytes 589824 | tf_op jit(solution)/shard_map/all_to_all | solution.py:234
  10.0 1.5 %collective-permute-start.4 = (bf16[128,2048]{1,0:T(8,128)(2,1)}, bf16[128,2048]{1,0:T(8,128)(2,1)}, u32[]{:S(2)}, u32[]{:S(2)}) collective-permute-start(bf16[128,2048]{1,0:T(8,128)(2,1)} %rest_0_.1), channel_id=1, source_target_pairs={{4,8},{5,9},{6,10},{7,11},{8,4},{9,5},{10,6},{11,7},{20,24},{21,25... | collective-permute-start | bytes 1572872 | tf_op jit(solution)/shard_map/ppermute | solution.py:153
  11.5 3.9 %collective-permute-start.1 = (bf16[128,2048]{1,0:T(8,128)(2,1)}, bf16[128,2048]{1,0:T(8,128)(2,1)S(1)}, u32[]{:S(2)}, u32[]{:S(2)}) collective-permute-start(bf16[128,2048]{1,0:T(8,128)(2,1)} %rest_0_.1), channel_id=1, source_target_pairs={{0,4},{1,5},{2,6},{3,7},{4,0},{5,1},{6,2},{7,3},{8,12},{9,13},{10,... | collective-permute-start | bytes 1572872 | tf_op jit(solution)/shard_map/ppermute | solution.py:153
  15.4 1.5 %collective-permute-start = (bf16[128,2048]{1,0:T(8,128)(2,1)}, bf16[128,2048]{1,0:T(8,128)(2,1)S(1)}, u32[]{:S(2)}, u32[]{:S(2)}) collective-permute-start(bf16[128,2048]{1,0:T(8,128)(2,1)} %rest_0_.1), channel_id=1, source_target_pairs={{0,2},{1,3},{2,0},{3,1},{4,6},{5,7},{6,4},{7,5},{8,10},{9,11},{10,... | collective-permute-start | bytes 1572872 | tf_op jit(solution)/shard_map/ppermute | solution.py:153
  16.8 1.3 %copy.12 = bf16[1,16,16,1024]{3,1,2,0:T(8,128)(2,1)S(1)} copy(bf16[1,16,16,1024]{3,2,1,0:T(8,128)(2,1)} %amps_ref.1) | data formatting | bytes 1048576 | tf_op args[0]
  18.2 0.0 copy-start
  18.2 0.0 collective-permute-done.4
  18.2 1.4 %collective-permute-start.5 = (bf16[128,2048]{1,0:T(8,128)(2,1)}, bf16[128,2048]{1,0:T(8,128)(2,1)}, u32[]{:S(2)}, u32[]{:S(2)}) collective-permute-start(bf16[128,2048]{1,0:T(8,128)(2,1)} %collective-permute-done.4), channel_id=1, source_target_pairs={{4,0},{5,1},{6,2},{7,3},{8,12},{9,13},{10,14},{11,15},{20,16},{21,... | collective-permute-start | bytes 1572872 | tf_op jit(solution)/shard_map/ppermute | solution.py:153
  19.6 9.6 %collective-permute-done.1.rest_1_ = bf16[128,2048]{1,0:T(8,128)(2,1)S(1)} collective-permute-done((bf16[128,2048]{1,0:T(8,128)(2,1)}, bf16[128,2048]{1,0:T(8,128)(2,1)S(1)}, u32[]{:S(2)}, u32[]{:S(2)}) %collective-permute-start.1) | collective-permute-done | bytes 524320 | tf_op jit(solution)/shard_map/ppermute | solution.py:153
  29.2 1.5 %collective-permute-start.3 = (bf16[128,2048]{1,0:T(8,128)(2,1)S(1)}, bf16[128,2048]{1,0:T(8,128)(2,1)}, u32[]{:S(2)}, u32[]{:S(2)}) collective-permute-start(bf16[128,2048]{1,0:T(8,128)(2,1)S(1)} %collective-permute-done.1.rest_1_), channel_id=1, source_target_pairs={{4,8},{5,9},{6,10},{7,11},{8,4},{9,5},{10,6},{11,7},{20,24},{21,25... | collective-permute-start | bytes 1572872 | tf_op jit(solution)/shard_map/ppermute | solution.py:153
  30.7 0.2 slice_reduce_fusion
  30.9 1.4 %gather_fusion = bf16[16,16,1024]{2,1,0:T(8,128)(2,1)} fusion(bf16[16,16,1024]{2,1,0:T(8,128)(2,1)S(1)} %bitcast.15, s32[1024]{0:T(1024)S(1)} %pad_clamp_fusion), kind=kCustom, calls=%fused_computation | custom fusion | bytes 1048640 | tf_op jit(solution)/shard_map/jit(_take)/gather | solution.py:238
  32.3 0.0 collective-permute-done.rest_4_
  32.3 9.3 %all-to-all-start.1 = ((bf16[16,16,1024]{2,1,0:T(8,128)(2,1)}), bf16[16,16,1024]{2,1,0:T(8,128)(2,1)S(1)}, u32[]{:S(2)}, u32[]{:S(2)}) async-start(bf16[16,16,1024]{2,1,0:T(8,128)(2,1)} %gather_fusion), calls=%async_computation.1 | async-start | bytes 1048576 | tf_op jit(solution)/shard_map/all_to_all | solution.py:239
  41.6 0.5 collective-permute-start.9
  42.1 0.6 dynamic_slice.6
  43.3 0.2 collective-permute-start.10
  43.5 1.9 %collective-permute-start.2 = (bf16[128,2048]{1,0:T(8,128)(2,1)S(1)}, bf16[128,2048]{1,0:T(8,128)(2,1)}, u32[]{:S(2)}, u32[]{:S(2)}) collective-permute-start(bf16[128,2048]{1,0:T(8,128)(2,1)S(1)} %collective-permute-done.1.rest_1_), channel_id=1, source_target_pairs={{0,2},{1,3},{2,0},{3,1},{4,6},{5,7},{6,4},{7,5},{8,10},{9,11},{10,... | collective-permute-start | bytes 1572872 | tf_op jit(solution)/shard_map/ppermute | solution.py:153
  45.4 0.8 collective-permute-done.5
  46.2 1.3 %collective-permute-start.6 = (bf16[128,2048]{1,0:T(8,128)(2,1)}, bf16[128,2048]{1,0:T(8,128)(2,1)}, u32[]{:S(2)}, u32[]{:S(2)}) collective-permute-start(bf16[128,2048]{1,0:T(8,128)(2,1)} %collective-permute-done.3), channel_id=1, source_target_pairs={{4,0},{5,1},{6,2},{7,3},{8,12},{9,13},{10,14},{11,15},{20,16},{21,... | collective-permute-start | bytes 1572872 | tf_op jit(solution)/shard_map/ppermute | solution.py:153
  47.5 1.1 %broadcast_select_fusion.1.rest_2_ = bf16[128,2048]{1,0:T(8,128)(2,1)S(1)} fusion(bf16[128,2048]{1,0:T(8,128)(2,1)} %collective-permute-done.5, bf16[128,2048]{1,0:T(8,128)(2,1)} %collective-permute-done.4, pred[]{:T(512)} %bitcast.6), kind=kLoop, calls=%fused_computation.3 | loop fusion | flops 262144 | bytes 1572865 | tf_op jit(solution)/shard_map/jit(_where)/select_n | solution.py:159
  48.6 9.3 %all-to-all-done.1.arrived_ref = bf16[16,16,1024]{2,1,0:T(8,128)(2,1)S(1)} async-done(((bf16[16,16,1024]{2,1,0:T(8,128)(2,1)}), bf16[16,16,1024]{2,1,0:T(8,128)(2,1)S(1)}, u32[]{:S(2)}, u32[]{:S(2)}) %all-to-all-start.1) | async-done | bytes 524320 | tf_op jit(solution)/shard_map/all_to_all | solution.py:239
  57.9 1.6 %copy-done.1 = bf16[1,1024,1024]{2,1,0:T(8,128)(2,1)S(1)} copy-done((bf16[1,1024,1024]{2,1,0:T(8,128)(2,1)S(1)}, bf16[1,1024,1024]{2,1,0:T(8,128)(2,1)}, u32[]{:S(2)}) %copy-start.1) | copy-done | bytes 2097176
  59.5 2.0 %shard_map.73 = bf16[16,24,1024]{2,1,0:T(8,128)(2,1)} custom-call(bf16[16,16,1024]{2,1,0:T(8,128)(2,1)S(1)} %all-to-all-done.1.arrived_ref, bf16[1,1024,1024]{2,1,0:T(8,128)(2,1)S(1)} %copy-done.1, bf16[1,16,16,1024]{3,2,1,0:T(8,128)(2,1)S(1)} %copy-done), custom_call_target="tpu_custom_call" | custom-call | flops 536870912 | bytes 2097152 | tf_op jit(solution)/shard_map/pallas_call | solution.py:63
  61.5 0.2 collective-permute-done.2.rest_5_
  61.7 1.6 %collective-permute-start.7 = (bf16[128,2048]{1,0:T(8,128)(2,1)S(1)}, bf16[128,2048]{1,0:T(8,128)(2,1)}, u32[]{:S(2)}, u32[]{:S(2)}) collective-permute-start(bf16[128,2048]{1,0:T(8,128)(2,1)S(1)} %broadcast_select_fusion.1.rest_2_), channel_id=1, source_target_pairs={{0,2},{1,3},{2,0},{3,1},{4,6},{5,7},{6,4},{7,5},{8,10},{9,11},{10,... | collective-permute-start | bytes 1572872 | tf_op jit(solution)/shard_map/ppermute | solution.py:153
  63.4 5.3 %all-to-all-start.2 = ((bf16[16,24,1024]{2,1,0:T(8,128)(2,1)}), bf16[16,24,1024]{2,1,0:T(8,128)(2,1)}, u32[]{:S(2)}, u32[]{:S(2)}) async-start(bf16[16,24,1024]{2,1,0:T(8,128)(2,1)} %shard_map.73), calls=%async_computation.2 | async-start | bytes 1572864 | tf_op jit(solution)/shard_map/all_to_all | solution.py:241
  68.7 1.1 %broadcast_select_fusion.rest_3_ = bf16[128,2048]{1,0:T(8,128)(2,1)S(1)} fusion(bf16[128,2048]{1,0:T(8,128)(2,1)} %collective-permute-done.6, bf16[128,2048]{1,0:T(8,128)(2,1)} %collective-permute-done.3, pred[]{:T(512)} %bitcast.6), kind=kLoop, calls=%fused_computation.2 | loop fusion | flops 262144 | bytes 1572865 | tf_op jit(solution)/shard_map/jit(_where)/select_n | solution.py:159
  69.8 1.9 %collective-permute-start.8 = (bf16[128,2048]{1,0:T(8,128)(2,1)S(1)}, bf16[128,2048]{1,0:T(8,128)(2,1)S(1)}, u32[]{:S(2)}, u32[]{:S(2)}) collective-permute-start(bf16[128,2048]{1,0:T(8,128)(2,1)S(1)} %broadcast_select_fusion.rest_3_), channel_id=1, source_target_pairs={{0,2},{1,3},{2,0},{3,1},{4,6},{5,7},{6,4},{7,5},{8,10},{9,11},{10,... | collective-permute-start | bytes 1572872 | tf_op jit(solution)/shard_map/ppermute | solution.py:153
  71.7 0.5 collective-permute-start.14
  72.3 0.1 collective-permute-start.12
  72.3 6.3 %collective-permute-done.7.rest_6_ = bf16[128,2048]{1,0:T(8,128)(2,1)} collective-permute-done((bf16[128,2048]{1,0:T(8,128)(2,1)S(1)}, bf16[128,2048]{1,0:T(8,128)(2,1)}, u32[]{:S(2)}, u32[]{:S(2)}) %collective-permute-start.7) | collective-permute-done | bytes 524320 | tf_op jit(solution)/shard_map/ppermute | solution.py:153
  78.7 3.4 %collective-permute-start.15 = (bf16[128,2048]{1,0:T(8,128)(2,1)}, bf16[128,2048]{1,0:T(8,128)(2,1)S(1)}, u32[]{:S(2)}, u32[]{:S(2)}) collective-permute-start(bf16[128,2048]{1,0:T(8,128)(2,1)} %collective-permute-done.7.rest_6_), channel_id=1, source_target_pairs={{0,1},{1,0},{2,3},{3,2},{4,5},{5,4},{6,7},{7,6},{8,9},{9,8},{10,11... | collective-permute-start | bytes 1572872 | tf_op jit(solution)/shard_map/ppermute | solution.py:153
  82.0 12.9 %collective-permute-done.8.rest_7_ = bf16[128,2048]{1,0:T(8,128)(2,1)S(1)} collective-permute-done((bf16[128,2048]{1,0:T(8,128)(2,1)S(1)}, bf16[128,2048]{1,0:T(8,128)(2,1)S(1)}, u32[]{:S(2)}, u32[]{:S(2)}) %collective-permute-start.8) | collective-permute-done | bytes 524320 | tf_op jit(solution)/shard_map/ppermute | solution.py:153
  95.0 1.0 collective-permute-start.16
  96.1 0.8 copy-done.7
  96.8 0.2 copy-done.8
  97.0 0.2 copy-done.10
  97.2 0.5 collective-permute-done.16.rest_15_
  97.7 0.3 copy-done.9
  98.0 8.8 %shard_map.74 = bf16[16,16,1024]{2,1,0:T(8,128)(2,1)} custom-call(s32[1]{0:T(128)} %bitcast.me, s32[16,16]{1,0:T(8,128)S(1)} %copy-done.3, s32[16]{0:T(128)S(1)} %get-tuple-element.10.targets, bf16[16,8,1152]{2,1,0:T(8,128)(2,1)S(1)} %all-to-all-done.ahead_ref, bf16[16,24,1024]{2,1,0:T(8,128)(2,1)} %all-to-all-done.2.moved_ref, ...), custom_call_target="tpu_custom_call" | custom-call | flops 1073741824 | bytes 8388608 | tf_op jit(solution)/shard_map/pallas_call | solution.py:126
  (32 shorter events, 0.1 us)
Async XLA Ops:
  1.8 39.8 %copy-start.2 = (bf16[128,2048]{1,0:T(8,128)(2,1)S(1)}, bf16[128,2048]{1,0:T(8,128)(2,1)}, u32[]{:S(2)}) copy-start(bf16[128,2048]{1,0:T(8,128)(2,1)} %rest_0_.1) | copy-start | bytes 1572868
  1.8 40.3 %copy-start.11 = (s32[16]{0:T(128)S(1)}, s32[16]{0:T(128)}, u32[]{:S(2)}) copy-start(s32[16]{0:T(128)} %constant.16.clone) | copy-start | bytes 196
  2.6 28.1 %all-to-all-start = ((bf16[16,8,1152]{2,1,0:T(8,128)(2,1)}), bf16[16,8,1152]{2,1,0:T(8,128)(2,1)S(1)}, u32[]{:S(2)}, u32[]{:S(2)}) async-start(bf16[16,8,1152]{2,1,0:T(8,128)(2,1)} %pad_maximum_fusion), calls=%async_computation | async-start | bytes 589824 | tf_op jit(solution)/shard_map/all_to_all | solution.py:234
  10.0 8.2 %collective-permute-start.4 = (bf16[128,2048]{1,0:T(8,128)(2,1)}, bf16[128,2048]{1,0:T(8,128)(2,1)}, u32[]{:S(2)}, u32[]{:S(2)}) collective-permute-start(bf16[128,2048]{1,0:T(8,128)(2,1)} %rest_0_.1), channel_id=1, source_target_pairs={{4,8},{5,9},{6,10},{7,11},{8,4},{9,5},{10,6},{11,7},{20,24},{21,25... | collective-permute-start | bytes 1572872 | tf_op jit(solution)/shard_map/ppermute | solution.py:153
  11.5 17.7 %collective-permute-start.1 = (bf16[128,2048]{1,0:T(8,128)(2,1)}, bf16[128,2048]{1,0:T(8,128)(2,1)S(1)}, u32[]{:S(2)}, u32[]{:S(2)}) collective-permute-start(bf16[128,2048]{1,0:T(8,128)(2,1)} %rest_0_.1), channel_id=1, source_target_pairs={{0,4},{1,5},{2,6},{3,7},{4,0},{5,1},{6,2},{7,3},{8,12},{9,13},{10,... | collective-permute-start | bytes 1572872 | tf_op jit(solution)/shard_map/ppermute | solution.py:153
  15.4 16.9 %collective-permute-start = (bf16[128,2048]{1,0:T(8,128)(2,1)}, bf16[128,2048]{1,0:T(8,128)(2,1)S(1)}, u32[]{:S(2)}, u32[]{:S(2)}) collective-permute-start(bf16[128,2048]{1,0:T(8,128)(2,1)} %rest_0_.1), channel_id=1, source_target_pairs={{0,2},{1,3},{2,0},{3,1},{4,6},{5,7},{6,4},{7,5},{8,10},{9,11},{10,... | collective-permute-start | bytes 1572872 | tf_op jit(solution)/shard_map/ppermute | solution.py:153
  18.2 39.8 %copy-start = (bf16[1,16,16,1024]{3,2,1,0:T(8,128)(2,1)S(1)}, bf16[1,16,16,1024]{3,2,1,0:T(8,128)(2,1)}, u32[]{:S(2)}) copy-start(bf16[1,16,16,1024]{3,2,1,0:T(8,128)(2,1)} %amps_ref.1) | copy-start | bytes 1572868
  18.2 28.0 %collective-permute-start.5 = (bf16[128,2048]{1,0:T(8,128)(2,1)}, bf16[128,2048]{1,0:T(8,128)(2,1)}, u32[]{:S(2)}, u32[]{:S(2)}) collective-permute-start(bf16[128,2048]{1,0:T(8,128)(2,1)} %collective-permute-done.4), channel_id=1, source_target_pairs={{4,0},{5,1},{6,2},{7,3},{8,12},{9,13},{10,14},{11,15},{20,16},{21,... | collective-permute-start | bytes 1572872 | tf_op jit(solution)/shard_map/ppermute | solution.py:153
  29.2 17.0 %collective-permute-start.3 = (bf16[128,2048]{1,0:T(8,128)(2,1)S(1)}, bf16[128,2048]{1,0:T(8,128)(2,1)}, u32[]{:S(2)}, u32[]{:S(2)}) collective-permute-start(bf16[128,2048]{1,0:T(8,128)(2,1)S(1)} %collective-permute-done.1.rest_1_), channel_id=1, source_target_pairs={{4,8},{5,9},{6,10},{7,11},{8,4},{9,5},{10,6},{11,7},{20,24},{21,25... | collective-permute-start | bytes 1572872 | tf_op jit(solution)/shard_map/ppermute | solution.py:153
  32.3 29.2 %copy-start.5 = (bf16[128,2048]{1,0:T(8,128)(2,1)}, bf16[128,2048]{1,0:T(8,128)(2,1)S(1)}, u32[]{:S(2)}) copy-start(bf16[128,2048]{1,0:T(8,128)(2,1)S(1)} %collective-permute-done.rest_4_) | copy-start | bytes 1572868
  32.3 25.6 %all-to-all-start.1 = ((bf16[16,16,1024]{2,1,0:T(8,128)(2,1)}), bf16[16,16,1024]{2,1,0:T(8,128)(2,1)S(1)}, u32[]{:S(2)}, u32[]{:S(2)}) async-start(bf16[16,16,1024]{2,1,0:T(8,128)(2,1)} %gather_fusion), calls=%async_computation.1 | async-start | bytes 1048576 | tf_op jit(solution)/shard_map/all_to_all | solution.py:239
  41.6 30.1 %collective-permute-start.9 = (bf16[128,2048]{1,0:T(8,128)(2,1)S(1)}, bf16[128,2048]{1,0:T(8,128)(2,1)}, u32[]{:S(2)}, u32[]{:S(2)}) collective-permute-start(bf16[128,2048]{1,0:T(8,128)(2,1)S(1)} %copy-done.2), channel_id=1, source_target_pairs={{0,1},{1,0},{2,3},{3,2},{4,5},{5,4},{6,7},{7,6},{8,9},{9,8},{10,11... | collective-permute-start | bytes 1572872 | tf_op jit(solution)/shard_map/ppermute | solution.py:153
  43.3 28.4 %collective-permute-start.10 = (bf16[128,2048]{1,0:T(8,128)(2,1)S(1)}, bf16[128,2048]{1,0:T(8,128)(2,1)}, u32[]{:S(2)}, u32[]{:S(2)}) collective-permute-start(bf16[128,2048]{1,0:T(8,128)(2,1)S(1)} %collective-permute-done.1.rest_1_), channel_id=1, source_target_pairs={{0,1},{1,0},{2,3},{3,2},{4,5},{5,4},{6,7},{7,6},{8,9},{9,8},{10,11... | collective-permute-start | bytes 1572872 | tf_op jit(solution)/shard_map/ppermute | solution.py:153
  43.5 18.2 %collective-permute-start.2 = (bf16[128,2048]{1,0:T(8,128)(2,1)S(1)}, bf16[128,2048]{1,0:T(8,128)(2,1)}, u32[]{:S(2)}, u32[]{:S(2)}) collective-permute-start(bf16[128,2048]{1,0:T(8,128)(2,1)S(1)} %collective-permute-done.1.rest_1_), channel_id=1, source_target_pairs={{0,2},{1,3},{2,0},{3,1},{4,6},{5,7},{6,4},{7,5},{8,10},{9,11},{10,... | collective-permute-start | bytes 1572872 | tf_op jit(solution)/shard_map/ppermute | solution.py:153
  46.2 26.1 %collective-permute-start.13 = (bf16[128,2048]{1,0:T(8,128)(2,1)S(1)}, bf16[128,2048]{1,0:T(8,128)(2,1)}, u32[]{:S(2)}, u32[]{:S(2)}) collective-permute-start(bf16[128,2048]{1,0:T(8,128)(2,1)S(1)} %collective-permute-done.rest_4_), channel_id=1, source_target_pairs={{0,1},{1,0},{2,3},{3,2},{4,5},{5,4},{6,7},{7,6},{8,9},{9,8},{10,11... | collective-permute-start | bytes 1572872 | tf_op jit(solution)/shard_map/ppermute | solution.py:153
  46.2 22.5 %collective-permute-start.6 = (bf16[128,2048]{1,0:T(8,128)(2,1)}, bf16[128,2048]{1,0:T(8,128)(2,1)}, u32[]{:S(2)}, u32[]{:S(2)}) collective-permute-start(bf16[128,2048]{1,0:T(8,128)(2,1)} %collective-permute-done.3), channel_id=1, source_target_pairs={{4,0},{5,1},{6,2},{7,3},{8,12},{9,13},{10,14},{11,15},{20,16},{21,... | collective-permute-start | bytes 1572872 | tf_op jit(solution)/shard_map/ppermute | solution.py:153
  57.9 1.6 %copy-start.1 = (bf16[1,1024,1024]{2,1,0:T(8,128)(2,1)S(1)}, bf16[1,1024,1024]{2,1,0:T(8,128)(2,1)}, u32[]{:S(2)}) copy-start(bf16[1,1024,1024]{2,1,0:T(8,128)(2,1)} %ints_ref.1) | copy-start | bytes 6291460
  61.5 36.5 %copy-start.3 = (s32[16,16]{1,0:T(8,128)S(1)}, s32[16,16]{1,0:T(8,128)}, u32[]{:S(2)}) copy-start(s32[16,16]{1,0:T(8,128)} %constant.17.clone.table) | copy-start | bytes 3076
  61.7 16.9 %collective-permute-start.7 = (bf16[128,2048]{1,0:T(8,128)(2,1)S(1)}, bf16[128,2048]{1,0:T(8,128)(2,1)}, u32[]{:S(2)}, u32[]{:S(2)}) collective-permute-start(bf16[128,2048]{1,0:T(8,128)(2,1)S(1)} %broadcast_select_fusion.1.rest_2_), channel_id=1, source_target_pairs={{0,2},{1,3},{2,0},{3,1},{4,6},{5,7},{6,4},{7,5},{8,10},{9,11},{10,... | collective-permute-start | bytes 1572872 | tf_op jit(solution)/shard_map/ppermute | solution.py:153
  63.4 34.3 %all-to-all-start.2 = ((bf16[16,24,1024]{2,1,0:T(8,128)(2,1)}), bf16[16,24,1024]{2,1,0:T(8,128)(2,1)}, u32[]{:S(2)}, u32[]{:S(2)}) async-start(bf16[16,24,1024]{2,1,0:T(8,128)(2,1)} %shard_map.73), calls=%async_computation.2 | async-start | bytes 1572864 | tf_op jit(solution)/shard_map/all_to_all | solution.py:241
  69.8 27.9 %copy-start.4 = (bf16[128,2048]{1,0:T(8,128)(2,1)}, bf16[128,2048]{1,0:T(8,128)(2,1)S(1)}, u32[]{:S(2)}) copy-start(bf16[128,2048]{1,0:T(8,128)(2,1)S(1)} %broadcast_select_fusion.rest_3_) | copy-start | bytes 1572868
  69.8 25.2 %collective-permute-start.8 = (bf16[128,2048]{1,0:T(8,128)(2,1)S(1)}, bf16[128,2048]{1,0:T(8,128)(2,1)S(1)}, u32[]{:S(2)}, u32[]{:S(2)}) collective-permute-start(bf16[128,2048]{1,0:T(8,128)(2,1)S(1)} %broadcast_select_fusion.rest_3_), channel_id=1, source_target_pairs={{0,2},{1,3},{2,0},{3,1},{4,6},{5,7},{6,4},{7,5},{8,10},{9,11},{10,... | collective-permute-start | bytes 1572872 | tf_op jit(solution)/shard_map/ppermute | solution.py:153
  71.7 24.3 %collective-permute-start.11 = (bf16[128,2048]{1,0:T(8,128)(2,1)S(1)}, bf16[128,2048]{1,0:T(8,128)(2,1)S(1)}, u32[]{:S(2)}, u32[]{:S(2)}) collective-permute-start(bf16[128,2048]{1,0:T(8,128)(2,1)S(1)} %broadcast_select_fusion.1.rest_2_), channel_id=1, source_target_pairs={{0,1},{1,0},{2,3},{3,2},{4,5},{5,4},{6,7},{7,6},{8,9},{9,8},{10,11... | collective-permute-start | bytes 1572872 | tf_op jit(solution)/shard_map/ppermute | solution.py:153
  71.7 24.3 %collective-permute-start.14 = (bf16[128,2048]{1,0:T(8,128)(2,1)}, bf16[128,2048]{1,0:T(8,128)(2,1)S(1)}, u32[]{:S(2)}, u32[]{:S(2)}) collective-permute-start(bf16[128,2048]{1,0:T(8,128)(2,1)} %collective-permute-done.2.rest_5_), channel_id=1, source_target_pairs={{0,1},{1,0},{2,3},{3,2},{4,5},{5,4},{6,7},{7,6},{8,9},{9,8},{10,11... | collective-permute-start | bytes 1572872 | tf_op jit(solution)/shard_map/ppermute | solution.py:153
  72.3 23.8 %collective-permute-start.12 = (bf16[128,2048]{1,0:T(8,128)(2,1)S(1)}, bf16[128,2048]{1,0:T(8,128)(2,1)S(1)}, u32[]{:S(2)}, u32[]{:S(2)}) collective-permute-start(bf16[128,2048]{1,0:T(8,128)(2,1)S(1)} %broadcast_select_fusion.rest_3_), channel_id=1, source_target_pairs={{0,1},{1,0},{2,3},{3,2},{4,5},{5,4},{6,7},{7,6},{8,9},{9,8},{10,11... | collective-permute-start | bytes 1572872 | tf_op jit(solution)/shard_map/ppermute | solution.py:153
  78.7 17.4 %collective-permute-start.15 = (bf16[128,2048]{1,0:T(8,128)(2,1)}, bf16[128,2048]{1,0:T(8,128)(2,1)S(1)}, u32[]{:S(2)}, u32[]{:S(2)}) collective-permute-start(bf16[128,2048]{1,0:T(8,128)(2,1)} %collective-permute-done.7.rest_6_), channel_id=1, source_target_pairs={{0,1},{1,0},{2,3},{3,2},{4,5},{5,4},{6,7},{7,6},{8,9},{9,8},{10,11... | collective-permute-start | bytes 1572872 | tf_op jit(solution)/shard_map/ppermute | solution.py:153
  95.0 1.1 %copy-start.6 = (bf16[128,2048]{1,0:T(8,128)(2,1)}, bf16[128,2048]{1,0:T(8,128)(2,1)S(1)}, u32[]{:S(2)}) copy-start(bf16[128,2048]{1,0:T(8,128)(2,1)S(1)} %collective-permute-done.8.rest_7_) | copy-start | bytes 1572868
  95.0 2.7 %collective-permute-start.16 = (bf16[128,2048]{1,0:T(8,128)(2,1)S(1)}, bf16[128,2048]{1,0:T(8,128)(2,1)}, u32[]{:S(2)}, u32[]{:S(2)}) collective-permute-start(bf16[128,2048]{1,0:T(8,128)(2,1)S(1)} %collective-permute-done.8.rest_7_), channel_id=1, source_target_pairs={{0,1},{1,0},{2,3},{3,2},{4,5},{5,4},{6,7},{7,6},{8,9},{9,8},{10,11... | collective-permute-start | bytes 1572872 | tf_op jit(solution)/shard_map/ppermute | solution.py:153
  96.0 0.8 copy-start.7
  96.0 1.0 copy-start.8
  96.0 1.1 %copy-start.10 = (bf16[128,2048]{1,0:T(8,128)(2,1)}, bf16[128,2048]{1,0:T(8,128)(2,1)S(1)}, u32[]{:S(2)}) copy-start(bf16[128,2048]{1,0:T(8,128)(2,1)S(1)} %collective-permute-done.15.rest_14_) | copy-start | bytes 1572868
  97.2 0.8 copy-start.9
